TPU v7x, 128 devices: a whole 4x4x4 slice. The times are simulated.
128 devices in a mesh: lat: 8 (over x, y_lo), ord: 16 (over y_hi, z, core).
Axes of the slice: x: 4, y: 4 (y_hi: 2, y_lo: 2; y = y_hi * 2 + y_lo), z: 4, core: 2. Of those that a mesh axis runs over, the one named last changes fastest.
Arguments:
- heights: bfloat16 [2048, 43200], P(('lat', 'ord')), may hold values from -1.5 to 1.5
- panels: bfloat16 [2048, 5120, 128], P('lat', 'ord'), may hold values from -0.125 to 0.125
- ord_slot: int32 [5120], replicated, may hold values from 0 to 5119, each once
- cutoffs: int32 [5120], P('ord'), may hold values from 13360 to 21599
Outputs:
- gravity: float32 [2048, 43200], P(('lat', 'ord'))
Inputs may be any that keep to these rules, and one draw needn't show every extreme that they name: `ord_slot`: a permutation of the order slots.
All inputs are finite; a program needn't handle non-finite values.
Results may differ from a plain program's by a relative error of at most 0.0039.
Values may be sent and summed in bfloat16 or wider, within the bound.
A program may use at most 192 MiB of HBM per device.

v0:
```python
import math

import jax
import jax.numpy as jnp
from jax import lax
from jax.sharding import PartitionSpec as P

LON_SLOW = 180
LON_FAST = 240
ORDERS = 5120
DEG = 128
NMAX = 21600


def slow_tables(slow):
    index = jnp.arange(slow, dtype=jnp.int32)
    phase = index[:, None] * index[None, :] % slow
    angle = 2.0 * math.pi / slow * phase.astype(jnp.float32)
    return (jnp.cos(angle), jnp.sin(angle))


def twiddle_tables(slow, fast, blocks):
    total = slow * fast
    first = jnp.arange(slow, dtype=jnp.int32)[:, None, None]
    middle = jnp.arange(fast, dtype=jnp.int32)[None, :, None]
    last = jnp.arange(blocks, dtype=jnp.int32)[None, None, :]
    phase = (middle * first + slow * middle * last) % total
    angle = 2.0 * math.pi / total * phase.astype(jnp.float32)
    return (jnp.cos(angle), jnp.sin(angle))


def forward_spectra(values, slow, fast, orders):
    count = values.shape[0]
    grid = values.reshape(count, slow, fast)
    cosine, sine = slow_tables(slow)
    first_real = jnp.einsum("raj,ak->rkj", grid, cosine, precision=lax.Precision.HIGHEST)
    first_imag = -jnp.einsum("raj,ak->rkj", grid, sine, precision=lax.Precision.HIGHEST)
    blocks = orders // slow + 1
    twist_cos, twist_sin = twiddle_tables(slow, fast, blocks)
    joined = jnp.concatenate([first_real, first_imag], 2)
    table = jnp.concatenate(
        [jnp.concatenate([twist_cos, -twist_sin], 2), jnp.concatenate([twist_sin, twist_cos], 2)], 1
    )
    second = jnp.einsum("rkj,kjq->rkq", joined, table, precision=lax.Precision.HIGHEST)
    scale_in = 1.0 / math.sqrt(slow * fast)
    spec_real = (
        second[:, :, :blocks].transpose(0, 2, 1).reshape(count, blocks * slow)[:, 1 : orders + 1]
    )
    spec_imag = (
        second[:, :, blocks:].transpose(0, 2, 1).reshape(count, blocks * slow)[:, 1 : orders + 1]
    )
    return (spec_real * scale_in, spec_imag * scale_in)


def inverse_field(full_real, full_imag, slow, fast):
    count = full_real.shape[0]
    blocks = full_real.shape[1] // slow
    grid_real = full_real.reshape(count, blocks, slow).transpose(0, 2, 1)
    grid_imag = full_imag.reshape(count, blocks, slow).transpose(0, 2, 1)
    joined = jnp.concatenate([grid_real, grid_imag], 2)
    twist_cos, twist_sin = twiddle_tables(slow, fast, blocks)
    cos_turned = twist_cos.transpose(0, 2, 1)
    sin_turned = twist_sin.transpose(0, 2, 1)
    table = jnp.concatenate(
        [
            jnp.concatenate([cos_turned, sin_turned], 2),
            jnp.concatenate([-sin_turned, cos_turned], 2),
        ],
        1,
    )
    second = jnp.einsum("rkq,kqj->rkj", joined, table, precision=lax.Precision.HIGHEST)
    cosine, sine = slow_tables(slow)
    field = jnp.einsum("rkj,ka->raj", second[:, :, :fast], cosine, precision=lax.Precision.HIGHEST)
    field = field - jnp.einsum(
        "rkj,ka->raj", second[:, :, fast:], sine, precision=lax.Precision.HIGHEST
    )
    return field.reshape(count, slow * fast)


def fold_powers(terms, factors):
    slots = terms.shape[1]
    width = terms.shape[2]
    return jnp.sum(terms.reshape(3, 2, slots, width) * factors[:, None, None, :], axis=0)


def local(heights, panels, ord_slot, cutoffs):
    lat_count = lax.axis_size("lat")
    ord_count = lax.axis_size("ord")
    level = heights.astype(jnp.float32)
    cycle_dev = level.shape[0]
    square = level * level
    powers = jnp.concatenate([level, square, square * level], 0)
    spec_real, spec_imag = forward_spectra(powers, LON_SLOW, LON_FAST, ORDERS)
    picked = jnp.stack(
        [
            spec_real[:, ord_slot].reshape(3, cycle_dev, ORDERS),
            spec_imag[:, ord_slot].reshape(3, cycle_dev, ORDERS),
        ],
        1,
    )
    picked = picked.reshape(6, cycle_dev, ORDERS).astype(jnp.bfloat16)
    sums = jnp.einsum(
        "xrk,rkn->xkn",
        lax.all_to_all(picked, "ord", split_axis=2, concat_axis=1, tiled=True),
        panels,
        preferred_element_type=jnp.float32,
    )
    stride = (NMAX - ORDERS) // DEG
    degree_int = ORDERS + jnp.arange(DEG, dtype=jnp.int32) * stride
    degree = degree_int.astype(jnp.float32)
    factors = jnp.stack(
        [
            jnp.ones_like(degree),
            (degree + 2.0) / (2.0 * NMAX),
            (degree + 2.0) * (degree + 1.0) / (6.0 * NMAX * NMAX),
        ]
    )
    keep = (degree_int[None, :] <= cutoffs[:, None]).astype(jnp.float32)
    total = lax.psum(sums, "lat")
    folded = fold_powers(total, factors)
    coeffs = (folded * keep[None]).astype(jnp.bfloat16)
    synthesis = jnp.einsum("rkn,ckn->crk", panels, coeffs, preferred_element_type=jnp.float32)
    returned = lax.all_to_all(synthesis, "ord", split_axis=1, concat_axis=2, tiled=True)
    blocks = ORDERS // LON_SLOW + 1
    target = ord_slot + 1
    full_real = (
        jnp.zeros((cycle_dev, blocks * LON_SLOW), jnp.float32).at[:, target].set(returned[0])
    )
    full_imag = (
        jnp.zeros((cycle_dev, blocks * LON_SLOW), jnp.float32).at[:, target].set(returned[1])
    )
    field = inverse_field(full_real, full_imag, LON_SLOW, LON_FAST)
    cycles_all = cycle_dev * lat_count * ord_count
    return field * math.sqrt(cycles_all / (DEG * ORDERS))


def solution(mesh):
    return jax.shard_map(
        local,
        mesh=mesh,
        in_specs=(P(("lat", "ord"), None), P("lat", "ord", None), P(), P("ord")),
        out_specs=P(("lat", "ord"), None),
        check_vma=False,
    )
```

profile of v0, /device:TPU:1, one launch (start us, length us, event | category | flops | bytes accessed | tf_op | source)
XLA Modules:
  0.0 490.3 jit_solution(14561908962304863775)
XLA Ops:
  8.5 3.5 pad_maximum_fusion.1
  12.1 11.4 %reshape.129 = f32[48,180,240]{2,1,0:T(8,128)} reshape(f32[48,43200]{1,0:T(8,128)} %pad_maximum_fusion.1) | data formatting | bytes 16588800 | tf_op jit(solution)/shard_map/reshape | solution.py:34
  23.5 13.3 %convolution_bitcast_fusion = f32[48,180,240]{2,1,0:T(8,128)S(1)} fusion(f32[48,180,240]{2,1,0:T(8,128)} %reshape.129), kind=kOutput, calls=%fused_computation.48 | convolution fusion | flops 4479267840 | bytes 16588800 | tf_op jit(solution)/shard_map/raj,ak->rkj/dot_general | solution.py:36
  36.8 9.9 %negate_bitcast_fusion = f32[48,180,240]{2,1,0:T(8,128)S(1)} fusion(f32[48,180,240]{2,1,0:T(8,128)S(1)} %copy-done), kind=kOutput, calls=%fused_computation.26 | convolution fusion | flops 4481341440 | bytes 16588800 | tf_op jit(solution)/shard_map/raj,ak->rkj/dot_general | solution.py:37
  46.8 7.9 %pad_maximum_fusion = f32[48,180,480]{2,1,0:T(8,128)} fusion(f32[48,180,240]{2,1,0:T(8,128)S(1)} %negate_bitcast_fusion, f32[48,180,240]{2,1,0:T(8,128)S(1)} %convolution_bitcast_fusion), kind=kLoop, calls=%fused_computation.24 | loop fusion | flops 4147200 | bytes 33177600 | tf_op jit(solution)/shard_map/concatenate | solution.py:40
  54.7 26.4 %fusion.50 = (f32[180,240,29]{1,2,0:T(8,128)}, f32[180,240,29]{1,2,0:T(8,128)}, f32[180,240,29]{1,2,0:T(8,128)}) fusion(s32[240,29]{0,1:T(8,128)S(1)} %iota_multiply_fusion.1, s32[180,240]{1,0:T(8,128)S(1)} %iota_multiply_fusion), kind=kLoop, calls=%fused_computation.59 | loop fusion | flops 12528000 | bytes 15234240 | tf_op jit(solution)/shard_map/neg | solution.py:42
  81.1 38.4 %fusion.42 = f32[48,180,58]{2,0,1:T(8,128)S(1)} fusion(f32[48,180,480]{2,1,0:T(8,128)} %pad_maximum_fusion, f32[180,240,29]{1,2,0:T(8,128)} %get-tuple-element.15, f32[180,240,29]{1,2,0:T(8,128)} %get-tuple-element.14, f32[180,240,29]{1,2,0:T(8,128)} %get-tuple-element.13), kind=kOutput, calls=%fused_computation.57 | convolution fusion | flops 2901484800 | bytes 33626880 | tf_op jit(solution)/shard_map/rkj,kjq->rkq/dot_general | solution.py:44
  119.5 4.8 slice_bitcast_fusion.1
  124.3 4.4 copy.110
  130.4 2.1 slice_multiply_fusion.1
  132.5 15.1 %gather_fusion = bf16[5120,48]{1,0:T(8,128)(2,1)S(1)} fusion(bf16[48,5120]{0,1:T(8,128)(2,1)S(1)} %slice_multiply_fusion.1, s32[5120]{0:T(1024)S(1)} %get-tuple-element.19), kind=kCustom, calls=%fused_computation | custom fusion | bytes 1003520 | tf_op jit(solution)/shard_map/gather | solution.py:96
  148.2 4.4 copy.111
  154.3 2.1 slice_multiply_fusion
  156.4 15.1 %gather_fusion.1 = bf16[5120,48]{1,0:T(8,128)(2,1)S(1)} fusion(bf16[48,5120]{0,1:T(8,128)(2,1)S(1)} %slice_multiply_fusion, s32[5120]{0:T(1024)S(1)} %get-tuple-element.19), kind=kCustom, calls=%fused_computation.1 | custom fusion | bytes 1003520 | tf_op jit(solution)/shard_map/gather | solution.py:97
  172.3 8.1 %copy.90 = bf16[6,16,5120]{1,0,2:T(8,128)(2,1)} copy(bf16[6,16,5120]{2,1,0:T(8,128)(2,1)S(1)} %bitcast.67) | data formatting | bytes 1966080 | tf_op jit(solution)/shard_map/convert_element_type | solution.py:101
  180.4 10.6 %reshape.179 = bf16[16,2,15360]{2,1,0:T(2,128)(2,1)S(1)} reshape(bf16[5120,6,16]{2,1,0:T(8,128)(2,1)} %bitcast.63) | data formatting | bytes 1966080
  191.1 25.5 %all_to_all.33 = bf16[16,2,15360]{2,1,0:T(2,128)(2,1)S(1)} all-to-all(bf16[16,2,15360]{2,1,0:T(2,128)(2,1)S(1)} %reshape.179), channel_id=1, replica_groups=mesh['lat'=8,'ord'=16] {'ord'}, dimensions={0} | all-to-all | bytes 1966080 | tf_op jit(solution)/shard_map/all_to_all | solution.py:104
  216.5 10.8 %reshape.180 = bf16[5120,6,16]{2,1,0:T(8,128)(2,1)} reshape(bf16[16,2,15360]{2,1,0:T(2,128)(2,1)S(1)} %all_to_all.33) | data formatting | bytes 1966080
  227.3 8.6 %copy.92 = bf16[6,16,16,320]{3,2,1,0:T(8,128)(2,1)S(1)} copy(bf16[6,16,16,320]{2,0,3,1:T(8,128)(2,1)} %bitcast.64) | data formatting | bytes 1966080 | tf_op jit(solution)/shard_map/all_to_all | solution.py:104
  237.2 27.0 %fusion.54 = f32[6,320,128]{2,0,1:T(8,128)S(1)} fusion(bf16[6,256,320]{1,0,2:T(8,128)(2,1)S(1)} %copy.93, bf16[256,320,128]{2,1,0:T(8,128)(2,1)} %param.5), kind=kOutput, calls=%fused_computation.63 | convolution fusion | flops 125829120 | bytes 22937600 | tf_op jit(solution)/shard_map/xrk,rkn->xkn/dot_general | solution.py:102
  265.6 69.9 %all-reduce.2.cloned.1.call-done = f32[3,2,320,128]{3,2,1,0:T(8,128)} async-done(((f32[3,2,320,128]{3,2,1,0:T(8,128)}), f32[3,2,320,128]{3,2,1,0:T(8,128)}) %all-reduce.2.cloned.1.call-update) | async-done | bytes 983056 | tf_op jit(solution)/shard_map/psum | solution.py:119
  336.8 28.5 %fusion.61 = f32[2,256,320]{1,0,2:T(2,128)S(1)} fusion(bf16[256,320,128]{2,1,0:T(8,128)(2,1)} %param.5, bf16[2,320,128]{2,1,0:T(8,128)(2,1)S(1)} %multiply_convert_fusion), kind=kOutput, calls=%fused_computation.72 | convolution fusion | flops 41943040 | bytes 21790720 | tf_op jit(solution)/shard_map/rkn,ckn->crk/dot_general | solution.py:122
  366.7 12.4 %all-to-all-start.1 = ((f32[2,256,320]{2,0,1:T(2,128)}), f32[2,256,320]{2,0,1:T(2,128)S(1)}, u32[]{:S(2)}, u32[]{:S(2)}) async-start(f32[2,256,320]{2,0,1:T(2,128)} %copy.98), calls=%async_computation.1 | async-start | bytes 1572864 | tf_op jit(solution)/shard_map/all_to_all | solution.py:123
  379.0 26.6 %fusion.31 = (f32[180,29,240]{2,1,0:T(8,128)}, f32[180,29,240]{2,1,0:T(8,128)}, f32[180,29,240]{2,1,0:T(8,128)}) fusion(s32[29,240]{1,0:T(8,128)S(1)} %iota_multiply_fusion.2, s32[180,240]{1,0:T(8,128)S(1)} %iota_multiply_fusion), kind=kLoop, calls=%fused_computation.42 | loop fusion | flops 12528000 | bytes 15234240 | tf_op jit(solution)/shard_map/sin | solution.py:29
  406.0 2.2 copy.101
  408.3 14.0 %scatter_custom_fusion = f32[16,5220]{0,1:T(8,128)S(1)} fusion(s32[5120]{0:T(1024)S(1)} %get-tuple-element.20, f32[5120,16]{1,0:T(8,128)} %copy.101, f32[]{:T(128)} %constant.52.clone.1), kind=kCustom, calls=%fused_computation.68 | custom fusion | bytes 334592 | tf_op jit(solution)/shard_map/scatter | solution.py:127
  426.0 2.2 copy.105
  428.3 14.0 %scatter_custom_fusion.1 = f32[16,5220]{0,1:T(8,128)S(1)} fusion(s32[5120]{0:T(1024)S(1)} %get-tuple-element.20, f32[5120,16]{1,0:T(8,128)} %copy.105, f32[]{:T(128)} %constant.52.clone.1), kind=kCustom, calls=%fused_computation.66 | custom fusion | bytes 334592 | tf_op jit(solution)/shard_map/scatter | solution.py:130
  445.8 23.8 %fusion.39 = f32[16,180,480]{2,0,1:T(8,128)S(1)} fusion(f32[180,29,240]{2,1,0:T(8,128)} %get-tuple-element.18, f32[180,29,240]{2,1,0:T(8,128)} %get-tuple-element.17, f32[180,29,240]{2,1,0:T(8,128)} %get-tuple-element.16, f32[16,180,29]{2,0,1:T(8,128)} %bitcast.74, f32[16,180,29]{2,0,1:T(8,128)} %bitcast.73), kind=kOutput, calls=%fused_computation.56 | convolution fusion | flops 977351040 | bytes 21231360 | tf_op jit(solution)/shard_map/rkq,kqj->rkj/dot_general | solution.py:71
  470.7 4.9 %fusion.35 = f32[180,16,240]{2,0,1:T(8,128)S(1)} fusion(f32[16,180,240]{2,0,1:T(8,128)S(1)} %get-tuple-element.6), kind=kOutput, calls=%fused_computation.49 | convolution fusion | flops 1493283584 | bytes 5529600 | tf_op jit(solution)/shard_map/rkj,ka->raj/dot_general | solution.py:74
  475.6 5.1 %multiply_bitcast_fusion = f32[16,180,240]{2,1,0:T(8,128)S(1)} fusion(f32[180,16,240]{2,0,1:T(8,128)S(1)} %fusion.35, f32[16,180,240]{2,0,1:T(8,128)S(1)} %get-tuple-element.5), kind=kOutput, calls=%fused_computation.53 | convolution fusion | flops 1494665984 | bytes 8294400 | tf_op jit(solution)/shard_map/rkj,ka->raj/dot_general | solution.py:73
  480.7 2.5 mul.334
  (47 shorter events, 20.5 us)
Async XLA Ops:
  6.5 1.8 copy-start.1
  6.5 328.9 %all-reduce.2.cloned.1.call-start = ((), (), s32[]{:S(2)}) async-start(), calls=%async_computation.2 | async-start | bytes 1966080 | tf_op jit(solution)/shard_map/psum | solution.py:119
  23.5 13.3 %copy-start = (f32[48,180,240]{2,1,0:T(8,128)S(1)}, f32[48,180,240]{2,1,0:T(8,128)}, u32[]{:S(2)}) copy-start(f32[48,180,240]{2,1,0:T(8,128)} %reshape.129) | copy-start | bytes 24883204
  128.7 3.8 copy-start.2
  237.2 28.3 %copy-start.3 = (s32[320]{0:T(512)S(1)}, s32[320]{0:T(512)}, u32[]{:S(2)}) copy-start(s32[320]{0:T(512)} %param.7) | copy-start | bytes 3844
  366.7 39.0 %all-to-all-start.1 = ((f32[2,256,320]{2,0,1:T(2,128)}), f32[2,256,320]{2,0,1:T(2,128)S(1)}, u32[]{:S(2)}, u32[]{:S(2)}) async-start(f32[2,256,320]{2,0,1:T(2,128)} %copy.98), calls=%async_computation.1 | async-start | bytes 1572864 | tf_op jit(solution)/shard_map/all_to_all | solution.py:123
Sparse Core Ops, SparseCore 0:
  265.5 69.8 all-reduce.1
where the time goes:
time: 497 us; the launch traced here: 490 us
  matrix products  151 us (30%)
  local copies, waits for them, and re-layouts  145 us (29%)
  other arithmetic  72.2 us (15%)
  waiting for transfers between devices  69.9 us (14%)
  blocking collectives  25.5 us (5%)
  between operations  14 us (3%)
  starting transfers between devices  12.4 us (2%)
    psum x1, waiting for transfers between devices, local(): total = lax.psum(sums, 'lat')  69.9 us
    dot_general x1, matrix products, forward_spectra(): jnp.einsum('rkj,kjq->rkq', joined, table, precision=lax.Precision.HIGHEST)  38.4 us
    scatter x4, local copies, waits for them, and re-layouts, local(): jnp.zeros((cycle_dev, blocks * LON_SLOW), jnp.float32).at[:, target]  29.5 us
    dot_general x1, matrix products, local(): jnp.einsum('rkn,ckn->crk', panels, coeffs, preferred_element_type=jnp.flo...  28.5 us
    dot_general x1, matrix products, local(): jnp.einsum('xrk,rkn->xkn', lax.all_to_all(picked, 'ord', split_axis=2, co...  27 us
    sin x1, other arithmetic, twiddle_tables(): return (jnp.cos(angle), jnp.sin(angle))  26.6 us
    neg x1, other arithmetic, forward_spectra(): -twist_sin  26.4 us
    all_to_all x1, blocking collectives, local(): lax.all_to_all(picked, 'ord', split_axis=2, concat_axis=1, tiled=True)  25.5 us
  transfers between devices with their start and end apart: 2, of which 1 were waited for; matrix products, arithmetic and copies ran while one was open for 5% of the time, Pallas kernels for 0%

commit v1 on v0

v1 whole, which is shorter than its diff:
```python
import functools
import math

import jax
import jax.numpy as jnp
import numpy as np
from jax import lax
from jax.experimental import pallas as pl
from jax.experimental.pallas import tpu as pltpu
from jax.sharding import PartitionSpec as P

LON = 43200
SLOW = 180
FAST = 240
HALF = 96
ORDERS = 5120
DEG = 128
NMAX = 21600
CYC = 16
TROWS = 6016
F32 = jnp.float32
BF16 = jnp.bfloat16
MIB = 1024 * 1024


def split16(table):
    high = table.astype(np.float32).astype(jnp.bfloat16)
    low = (table - high.astype(np.float64)).astype(np.float32).astype(jnp.bfloat16)
    return high, low


def angles(left, right, total):
    return 2.0 * np.pi / total * ((left[:, None] * right[None, :]) % total)


@functools.cache
def tables():
    k = np.arange(91)
    a = np.arange(SLOW)
    b = np.arange(FAST)
    q = np.arange(29)
    ka = angles(k, a, SLOW)
    first = np.zeros((2, HALF, 192))
    first[0, :91, :SLOW] = np.cos(ka)
    first[1, :91, :SLOW] = -np.sin(ka)
    first = first.reshape(2 * HALF, 192)
    kb = angles(k, b, LON)
    twist = np.zeros((2, HALF, 256), np.float32)
    twist[0, :91, :FAST] = np.cos(kb)
    twist[1, :91, :FAST] = np.sin(kb)
    bq = angles(b, q, FAST)
    bq1 = angles(b, q + 1, FAST)
    second = np.zeros((2, 256, 2, 128))
    second[0, :FAST, 0, 0:29] = np.cos(bq)
    second[1, :FAST, 0, 0:29] = np.sin(bq)
    second[0, :FAST, 1, 0:29] = -np.sin(bq)
    second[1, :FAST, 1, 0:29] = np.cos(bq)
    second[0, :FAST, 0, 32:61] = np.cos(bq1)
    second[1, :FAST, 0, 32:61] = -np.sin(bq1)
    second[0, :FAST, 1, 32:61] = -np.sin(bq1)
    second[1, :FAST, 1, 32:61] = -np.cos(bq1)
    second = second.reshape(512, 256) / math.sqrt(LON)
    back = np.zeros((2, 2, 32, 2, 256))
    back[0, 0, :29, 0, :FAST] = np.cos(bq).T
    back[0, 0, :29, 1, :FAST] = np.sin(bq).T
    back[1, 0, :29, 0, :FAST] = -np.sin(bq).T
    back[1, 0, :29, 1, :FAST] = np.cos(bq).T
    back[0, 1, :29, 0, :FAST] = np.cos(bq1).T
    back[0, 1, :29, 1, :FAST] = -np.sin(bq1).T
    back[1, 1, :29, 0, :FAST] = -np.sin(bq1).T
    back[1, 1, :29, 1, :FAST] = -np.cos(bq1).T
    back = np.concatenate(split16(back.reshape(128, 512)), 0)
    last = np.zeros((192, 2, HALF))
    last[:SLOW, 0, :91] = np.cos(ka).T
    last[:SLOW, 1, :91] = -np.sin(ka).T
    last = last.reshape(192, 2 * HALF) * math.sqrt(2048 / (DEG * ORDERS))
    rows = np.arange(128)
    lanes = np.arange(256)
    diag = (lanes[None, :] % 16 == rows[:, None] // 8).astype(jnp.bfloat16)
    pick = (lanes[None, :] % 16 == np.arange(32)[:, None] % 16).astype(np.float32)
    return dict(
        first=split16(first), twist=twist, second=split16(second), back=back,
        last=split16(last), diag=diag, pick=pick,
    )


def swap_chunks(rows):
    rows = list(rows)
    chunk = lax.broadcasted_iota(jnp.int32, (8, 128), 1) // 16
    for d in (4, 2, 1):
        low = (chunk & d) == 0
        new = list(rows)
        for r in range(8):
            if r & d:
                continue
            new[r] = jnp.where(low, rows[r], pltpu.roll(rows[r + d], d * 16, 1))
            new[r + d] = jnp.where(low, pltpu.roll(rows[r], 128 - d * 16, 1), rows[r + d])
        rows = new
    return rows


def dot(left, right):
    return jnp.dot(left, right, preferred_element_type=F32)


def halves(value):
    high = value.astype(BF16)
    return high, (value - high.astype(F32)).astype(BF16)


def forward_kernel(slot_ref, x_ref, fh_ref, fl_ref, twist_ref, sh_ref, sl_ref, out_ref,
                   xs, qs, ts, gs):
    keep = lax.broadcasted_iota(jnp.int32, (CYC, 256), 1) < FAST
    for r in range(CYC):
        for lane in range(2):
            xs[lane, r * 192 + 176 : r * 192 + 192, :] = jnp.zeros((16, 128), F32)
    for a in range(SLOW):
        start = FAST * a // 128 * 128
        off = FAST * a - start
        if start + 384 <= LON:
            v = x_ref[:, start : start + 384].astype(F32)
        else:
            v = jnp.concatenate(
                [x_ref[:, start:LON].astype(F32), jnp.zeros((CYC, start + 384 - LON), F32)], 1
            )
        if off:
            v = pltpu.roll(v, 384 - off, 1)
        v = jnp.where(keep, v[:, :256], 0.0)
        for lane in range(2):
            xs.at[lane][pl.ds(a, CYC, stride=192), :] = v[:, lane * 128 : lane * 128 + 128]

    def one_cycle(r, carry):
        rows = pl.ds(pl.multiple_of(r * 192, 192), 192)
        level = jnp.concatenate([xs[0, rows, :], xs[1, rows, :]], 1)
        value = level
        for p in range(3):
            if p:
                value = value * level
            if p == 0:
                high = value.astype(BF16)
                y = dot(fh_ref[...], high) + dot(fl_ref[...], high)
            else:
                high, low = halves(value)
                y = dot(fh_ref[...], high) + dot(fl_ref[...], high) + dot(fh_ref[...], low)
            re, im = y[:HALF], y[HALF:]
            c, s = twist_ref[0], twist_ref[1]
            z = jnp.concatenate([re * c + im * s, im * c - re * s], 1)
            zh, zl = halves(z)
            o = dot(zh, sh_ref[...]) + dot(zh, sl_ref[...]) + dot(zl, sh_ref[...])
            qs[pl.ds(r * 8 + p, HALF, stride=128), :] = o[:, :128]
            qs[pl.ds(r * 8 + 3 + p, HALF, stride=128), :] = o[:, 128:]
        for x in (6, 7):
            qs[pl.ds(r * 8 + x, HALF, stride=128), :] = jnp.zeros((HALF, 128), F32)
        return carry

    lax.fori_loop(0, CYC, one_cycle, 0)

    def one_k(k, carry):
        t = qs[pl.ds(pl.multiple_of(k * 128, 128), 128), :].T
        ts[pl.ds(k, 32, stride=SLOW), :] = t[0:32]
        ts[pl.ds(SLOW - k, 32, stride=SLOW), :] = t[32:64]
        return carry

    lax.fori_loop(0, 91, one_k, 0)

    def one_tile(tile, carry):
        for i in range(128):
            gs[i : i + 1, :] = ts[pl.ds(slot_ref[tile * 128 + i] + 1, 1), :]
        t = gs[...].T
        sides = []
        for h in range(2):
            sides.append(
                jnp.concatenate(swap_chunks([t[(h * 8 + r) * 8 : (h * 8 + r + 1) * 8] for r in range(8)]), 0)
            )
        out_ref[pl.ds(pl.multiple_of(tile * 64, 64), 64), :] = jnp.concatenate(sides, 1).astype(BF16)
        return carry

    lax.fori_loop(0, ORDERS // 128, one_tile, 0)


def vmem():
    return pl.BlockSpec(memory_space=pltpu.VMEM)


def forward(heights, slots):
    t = tables()
    return pl.pallas_call(
        forward_kernel,
        out_shape=jax.ShapeDtypeStruct((ORDERS // 2, 256), BF16),
        in_specs=[pl.BlockSpec(memory_space=pltpu.SMEM)] + [vmem()] * 6,
        out_specs=vmem(),
        scratch_shapes=[
            pltpu.VMEM((2, CYC * 192, 128), F32),
            pltpu.VMEM((HALF * 128, 128), F32),
            pltpu.VMEM((TROWS, 128), F32),
            pltpu.VMEM((128, 128), F32),
        ],
        compiler_params=pltpu.CompilerParams(vmem_limit_bytes=48 * MIB),
        name="forward",
    )(slots, heights, *t["first"], t["twist"], *t["second"])


def analysis_kernel(msg_ref, panel_ref, diag_ref, factor_ref, out_ref):
    step = pl.program_id(0)
    for pair in range(2):
        accs = [None, None]
        for R in range(16):
            both = msg_ref[pl.ds(pl.multiple_of(R * 160 + step * 32 + pair * 16, 16), 16), :]
            both = both.astype(F32)
            for e in range(2):
                one = both[e * 8 : e * 8 + 8]
                two = jnp.concatenate([one, one], 0).astype(BF16)
                left = jnp.concatenate([two] * 8, 0) * diag_ref[...]
                g = pair * 2 + e
                right = panel_ref[R * 16 : R * 16 + 16, g * 16 : g * 16 + 16, :].reshape(256, DEG)
                d = dot(left, right)
                accs[e] = d if accs[e] is None else accs[e] + d
        for e in range(2):
            g = pair * 2 + e
            acc = accs[e].reshape(16, 8, DEG)
            for c in range(2):
                out_ref[c, g * 16 : g * 16 + 16, :] = jnp.sum(acc * factor_ref[c][None], axis=1)


def analysis(msg, panels, factors):
    t = tables()
    return pl.pallas_call(
        analysis_kernel,
        grid=(5,),
        out_shape=jax.ShapeDtypeStruct((2, 320, DEG), F32),
        in_specs=[
            pl.BlockSpec((ORDERS // 2, 256), lambda i: (0, 0)),
            pl.BlockSpec((256, 64, DEG), lambda i: (0, i, 0)),
            pl.BlockSpec((128, 256), lambda i: (0, 0)),
            pl.BlockSpec((2, 8, DEG), lambda i: (0, 0, 0)),
        ],
        out_specs=pl.BlockSpec((2, 64, DEG), lambda i: (0, i, 0)),
        compiler_params=pltpu.CompilerParams(vmem_limit_bytes=48 * MIB),
        name="analysis",
    )(msg, panels, t["diag"], factors)


def synthesis_kernel(coeff_ref, panel_ref, pick_ref, out_ref):
    for g in range(4):
        left = jnp.concatenate([coeff_ref[c, g * 16 : g * 16 + 16, :] for c in range(2)], 0)
        for R in range(16):
            right = panel_ref[R * 16 : R * 16 + 16, g * 16 : g * 16 + 16, :].reshape(256, DEG)
            d = lax.dot_general(left, right, (((1,), (1,)), ((), ())), preferred_element_type=F32)
            d = d * pick_ref[...]
            out_ref[R, g * 2 : g * 2 + 1, :] = jnp.sum(d[:16], axis=0, keepdims=True)
            out_ref[R, g * 2 + 1 : g * 2 + 2, :] = jnp.sum(d[16:], axis=0, keepdims=True)


def synthesize(coeffs, panels):
    t = tables()
    return pl.pallas_call(
        synthesis_kernel,
        grid=(5,),
        out_shape=jax.ShapeDtypeStruct((16, 40, 256), F32),
        in_specs=[
            pl.BlockSpec((2, 64, DEG), lambda i: (0, i, 0)),
            pl.BlockSpec((256, 64, DEG), lambda i: (0, i, 0)),
            pl.BlockSpec((32, 256), lambda i: (0, 0)),
        ],
        out_specs=pl.BlockSpec((16, 8, 256), lambda i: (0, i, 0)),
        compiler_params=pltpu.CompilerParams(vmem_limit_bytes=48 * MIB),
        name="synthesis",
    )(coeffs, panels, t["pick"])


def inverse_kernel(slot_ref, msg_ref, back_ref, twist_ref, lh_ref, ll_ref, out_ref, ts, ls, ys):
    ts[0:8, :] = jnp.zeros((8, 128), F32)
    ts[ORDERS:TROWS, :] = jnp.zeros((TROWS - ORDERS, 128), F32)

    def one_peer(o, carry):
        for part in range(3):
            rows = msg_ref[pl.ds(pl.multiple_of(o * 48 + part * 16, 16), 16), :].astype(F32)
            count = 128 if part < 2 else 64
            blocks = []
            for h in range(2):
                side = rows[:, h * 128 : h * 128 + 128]
                groups = []
                for g in range(8):
                    v = side[g // 4 * 8 : g // 4 * 8 + 8]
                    if g % 4:
                        v = pltpu.roll(v, 8 - 2 * (g % 4), 0)
                    groups.append(v)
                blocks += swap_chunks(groups)
            t = jnp.concatenate(blocks, 0).T
            base = o * 320 + part * 128
            for i in range(count):
                ts[pl.ds(slot_ref[base + i] + 1, 1), :] = t[i : i + 1]
        return carry

    lax.fori_loop(0, 16, one_peer, 0)

    def one_k(k, carry):
        plus = ts[pl.ds(k, 32, stride=SLOW), :]
        minus = ts[pl.ds(SLOW - k, 32, stride=SLOW), :]
        minus = jnp.where(jnp.logical_and(k > 0, k < 90), minus, 0.0)
        both = jnp.concatenate([plus, minus, jnp.zeros((64, 128), F32)], 0)
        ls[pl.ds(k, 128, stride=HALF), :] = both.T
        return carry

    lax.fori_loop(0, HALF, one_k, 0)

    def one_cycle(r, carry):
        parts = []
        for c in range(2):
            parts.append(ls[pl.ds(pl.multiple_of((r * 8 + c) * HALF, HALF), HALF), :][:, :64])
        left = jnp.concatenate(parts, 1).astype(BF16)
        w = dot(jnp.concatenate([left, left], 1), back_ref[...])
        re, im = w[:, :256], w[:, 256:]
        c, s = twist_ref[0], twist_ref[1]
        v = jnp.concatenate([re * c - im * s, im * c + re * s], 0).astype(BF16)
        field = dot(lh_ref[...], v) + dot(ll_ref[...], v)
        for lane in range(2):
            ys[lane, pl.ds(pl.multiple_of(r * 192, 192), 192), :] = field[:, lane * 128 : lane * 128 + 128]
        return carry

    lax.fori_loop(0, CYC, one_cycle, 0)
    for a in range(SLOW):
        v = jnp.concatenate([ys.at[lane][pl.ds(a, CYC, stride=192), :] for lane in range(2)], 1)
        out_ref[:, FAST * a : FAST * a + FAST] = v[:, :FAST]


def inverse(msg, slots):
    t = tables()
    return pl.pallas_call(
        inverse_kernel,
        out_shape=jax.ShapeDtypeStruct((CYC, LON), F32),
        in_specs=[pl.BlockSpec(memory_space=pltpu.SMEM)] + [vmem()] * 5,
        out_specs=vmem(),
        scratch_shapes=[
            pltpu.VMEM((TROWS, 128), F32),
            pltpu.VMEM((128 * HALF, 128), F32),
            pltpu.VMEM((2, CYC * 192, 128), F32),
        ],
        compiler_params=pltpu.CompilerParams(vmem_limit_bytes=48 * MIB),
        name="inverse",
    )(slots, msg, t["back"], t["twist"], *t["last"])


def degrees():
    stride = (NMAX - ORDERS) // DEG
    return ORDERS + np.arange(DEG, dtype=np.int32) * stride


def factor_rows():
    degree = degrees().astype(np.float64)
    rows = np.zeros((2, 8, DEG), np.float32)
    for c in range(2):
        rows[c, 3 * c] = 1.0
        rows[c, 3 * c + 1] = (degree + 2.0) / (2.0 * NMAX)
        rows[c, 3 * c + 2] = (degree + 2.0) * (degree + 1.0) / (6.0 * NMAX * NMAX)
    return rows


def local(heights, panels, ord_slot, cutoffs):
    msg = forward(heights, ord_slot)
    got = lax.all_to_all(msg, "ord", split_axis=0, concat_axis=0, tiled=True)
    folded = lax.psum(analysis(got, panels, factor_rows()), "lat")
    keep = (degrees()[None, :] <= cutoffs[:, None]).astype(F32)
    coeffs = (folded * keep[None]).astype(BF16)
    synth = synthesize(coeffs, panels)
    synth = jnp.pad(synth.astype(BF16), ((0, 0), (0, 8), (0, 0))).reshape(16 * 48, 256)
    back = lax.all_to_all(synth, "ord", split_axis=0, concat_axis=0, tiled=True)
    return inverse(back, ord_slot)


def solution(mesh):
    return jax.shard_map(
        local,
        mesh=mesh,
        in_specs=(P(("lat", "ord"), None), P("lat", "ord", None), P(), P("ord")),
        out_specs=P(("lat", "ord"), None),
        check_vma=False,
    )
```

time: 497 us -> 240 us (0.48); the launches traced: 490 us -> 239 us
  matrix products: 151 us -> 0 us
  local copies, waits for them, and re-layouts: 145 us -> 6.77 us
  Pallas kernels: 0 us -> 99.9 us
  other arithmetic: 72.2 us -> 1.14 us
  blocking collectives: 25.5 us -> 51.6 us
  starting transfers between devices: 12.4 us -> 0.01 us
    dot_general x8 -> x0, matrix products: 151 us -> none  [the longest x1 38.4 us: forward_spectra(): jnp.einsum('rkj,kjq->rkq', joined, table, precision=lax.Precision.HIGHEST)]
    pallas_call x0 -> x4, Pallas kernels: none -> 99.9 us  [the longest x1 43.9 us: forward(): pl.pallas_call(forward_kernel, out_shape=jax.ShapeDtypeStruct((ORDERS //...]
    gather x2 -> x0, local copies, waits for them, and re-layouts: 30.2 us -> none  [the longest x1 15.1 us: local(): spec_real[:, ord_slot].reshape(3, cycle_dev, ORDERS)]
    scatter x4 -> x0, local copies, waits for them, and re-layouts: 29.5 us -> none  [local(): jnp.zeros((cycle_dev, blocks * LON_SLOW), jnp.float32).at[:, target]]
    reshape x9 -> x0, local copies, waits for them, and re-layouts: 29 us -> none  [the longest x1 11.4 us: forward_spectra(): grid = values.reshape(count, slow, fast)]
    sin x1 -> x0, other arithmetic: 26.6 us -> none  [twiddle_tables(): return (jnp.cos(angle), jnp.sin(angle))]
    neg x1 -> x0, other arithmetic: 26.4 us -> none  [forward_spectra(): -twist_sin]
    all_to_all x1 -> x2, blocking collectives: 25.5 us -> 51.6 us  [the longest x1 29.3 us: local(): got = lax.all_to_all(msg, 'ord', split_axis=0, concat_axis=0, tiled=True)]
  transfers between devices with their start and end apart: 2 -> 1, of which waited for: 1 -> 1; matrix products, arithmetic and copies ran while one was open for 5% -> 0% of each run, Pallas kernels for 0% -> 0%
where the time goes in v1:
time: 240 us; the launch traced here: 239 us
  Pallas kernels  99.9 us (42%)
  waiting for transfers between devices  66 us (28%)
  blocking collectives  51.6 us (22%)
  between operations  13.6 us (6%)
  local copies, waits for them, and re-layouts  6.77 us (3%)
    psum x1, waiting for transfers between devices, local(): folded = lax.psum(analysis(got, panels, factor_rows()), 'lat')  66 us
    pallas_call x1, Pallas kernels, forward(): pl.pallas_call(forward_kernel, out_shape=jax.ShapeDtypeStruct((ORDERS //...  43.9 us
    pallas_call x1, Pallas kernels, inverse(): pl.pallas_call(inverse_kernel, out_shape=jax.ShapeDtypeStruct((CYC, LON),...  32.9 us
    all_to_all x1, blocking collectives, local(): got = lax.all_to_all(msg, 'ord', split_axis=0, concat_axis=0, tiled=True)  29.3 us
    all_to_all x1, blocking collectives, local(): back = lax.all_to_all(synth, 'ord', split_axis=0, concat_axis=0, tiled=True)  22.3 us
    pallas_call x1, Pallas kernels, analysis(): pl.pallas_call(analysis_kernel, grid=(5,), out_shape=jax.ShapeDtypeStruct...  11.6 us
    pallas_call x1, Pallas kernels, synthesize(): pl.pallas_call(synthesis_kernel, grid=(5,), out_shape=jax.ShapeDtypeStruc...  11.4 us
    unnamed x34, local copies, waits for them, and re-layouts  6.74 us
  transfers between devices with their start and end apart: 1, of which 1 were waited for; matrix products, arithmetic and copies ran while one was open for 0% of the time, Pallas kernels for 0%

profile of v1, /device:TPU:1, one launch (start us, length us, event | category | flops | bytes accessed | tf_op | source)
XLA Modules:
  0.0 239.0 jit_solution(3659619376007773444)
XLA Ops:
  6.5 0.0 all-reduce.3.cloned.1.call-start
  6.5 1.3 copy-done
  7.9 0.9 copy-done.1
  8.8 0.9 copy-done.4
  9.8 0.9 copy-done.5
  10.7 0.9 copy-done.8
  11.6 0.9 copy-done.9
  12.5 0.7 copy-done.10
  13.2 43.9 %forward.1 = bf16[2560,256]{1,0:T(8,128)(2,1)S(1)} custom-call(s32[5120]{0:T(1024)S(1)} %copy-done.10, bf16[16,43200]{1,0:T(8,128)(2,1)S(1)} %copy-done, bf16[192,192]{1,0:T(8,128)(2,1)S(1)} %copy-done.9, bf16[192,192]{1,0:T(8,128)(2,1)S(1)} %copy-done.8, f32[2,96,256]{2,1,0:T(8,128)S(1)} %copy-done.1, bf16[512,256]{1,0:T(8,128)(2,1)S(1)} %copy-done.5, ...), custom_call_target="tpu_custom_call" | custom-call | tf_op jit(solution)/shard_map/forward/pallas_call | solution.py:187
  57.2 0.0 copy-start.12
  57.2 0.0 copy-start.14
  57.2 29.3 %all_to_all.19 = bf16[16,160,256]{2,1,0:T(8,128)(2,1)S(1)} all-to-all(bf16[16,160,256]{2,1,0:T(8,128)(2,1)S(1)} %bitcast.4), channel_id=1, replica_groups=mesh['lat'=8,'ord'=16] {'ord'}, dimensions={0} | all-to-all | bytes 2621440 | tf_op jit(solution)/shard_map/all_to_all | solution.py:361
  86.5 0.0 copy-done.12
  86.5 0.0 copy-done.14
  86.5 0.0 copy-start.13
  86.5 11.6 %analysis.1 = f32[2,320,128]{2,1,0:T(8,128)} custom-call(bf16[2560,256]{1,0:T(8,128)(2,1)S(1)} %bitcast.3, bf16[256,320,128]{2,1,0:T(8,128)(2,1)} %panel_ref.3, bf16[128,256]{1,0:T(8,128)(2,1)S(1)} %copy-done.12, f32[2,8,128]{2,1,0:T(8,128)S(1)} %copy-done.14), custom_call_target="tpu_custom_call" | custom-call | tf_op jit(solution)/shard_map/analysis/pallas_call | solution.py:227
  98.1 0.0 all-reduce.3.cloned.1.call-update
  98.1 0.0 copy-done.15
  98.1 0.0 copy-done.16
  98.1 0.1 compare_convert_fusion
  98.3 66.0 %all-reduce.3.cloned.1.call-done = f32[2,320,128]{2,1,0:T(8,128)} async-done(((f32[2,320,128]{2,1,0:T(8,128)}), f32[2,320,128]{2,1,0:T(8,128)}) %all-reduce.3.cloned.1.call-update) | async-done | bytes 327696 | tf_op jit(solution)/shard_map/psum | solution.py:362
  164.3 1.0 multiply_convert_fusion.coeff_ref
  165.3 11.4 %synthesis.1 = f32[16,40,256]{2,1,0:T(8,128)S(1)} custom-call(bf16[2,320,128]{2,1,0:T(8,128)(2,1)S(1)} %multiply_convert_fusion.coeff_ref, bf16[256,320,128]{2,1,0:T(8,128)(2,1)} %panel_ref.3, f32[32,256]{1,0:T(8,128)S(1)} %copy-done.13), custom_call_target="tpu_custom_call" | custom-call | tf_op jit(solution)/shard_map/synthesis/pallas_call | solution.py:256
  176.7 0.0 copy-start.2
  176.8 0.0 copy-start.3
  176.8 0.0 copy-start.6
  176.8 0.0 copy-start.7
  176.8 0.0 copy-start.11
  176.9 22.3 %all_to_all.20 = bf16[16,48,256]{2,1,0:T(8,128)(2,1)S(1)} all-to-all(bf16[16,48,256]{2,1,0:T(8,128)(2,1)S(1)} %pad.4), channel_id=1, replica_groups=mesh['lat'=8,'ord'=16] {'ord'}, dimensions={0} | all-to-all | bytes 786432 | tf_op jit(solution)/shard_map/all_to_all | solution.py:367
  199.2 0.0 copy-done.2
  199.2 0.0 copy-done.6
  199.3 32.9 %inverse.1 = f32[16,43200]{1,0:T(8,128)} custom-call(s32[5120]{0:T(1024)S(1)} %copy-done.11, bf16[768,256]{1,0:T(8,128)(2,1)S(1)} %bitcast.5, bf16[256,512]{1,0:T(8,128)(2,1)S(1)} %copy-done.3, f32[2,96,256]{2,1,0:T(8,128)S(1)} %copy-done.2, bf16[192,192]{1,0:T(8,128)(2,1)S(1)} %copy-done.7, bf16[192,192]{1,0:T(8,128)(2,1)S(1)} %copy-done.6), custom_call_target="tpu_custom_call" | custom-call | tf_op jit(solution)/shard_map/inverse/pallas_call | solution.py:329
  (15 shorter events, 0.1 us)
Async XLA Ops:
  6.5 157.7 %all-reduce.3.cloned.1.call-start = ((), (), s32[]{:S(2)}) async-start(), calls=%async_computation.2 | async-start | bytes 655360 | tf_op jit(solution)/shard_map/psum | solution.py:362
  6.5 1.3 copy-start
  7.9 0.9 copy-start.1
  8.8 0.9 copy-start.4
  9.8 0.9 copy-start.5
  10.7 0.9 copy-start.8
  11.6 0.9 copy-start.9
  12.5 0.7 copy-start.10
  57.2 29.3 %copy-start.12 = (bf16[128,256]{1,0:T(8,128)(2,1)S(1)}, bf16[128,256]{1,0:T(8,128)(2,1)}, u32[]{:S(2)}) copy-start(bf16[128,256]{1,0:T(8,128)(2,1)} %constant.32.clone.diag_ref) | copy-start | bytes 196612
  57.2 29.3 %copy-start.14 = (f32[2,8,128]{2,1,0:T(8,128)S(1)}, f32[2,8,128]{2,1,0:T(8,128)}, u32[]{:S(2)}) copy-start(f32[2,8,128]{2,1,0:T(8,128)} %constant.33.clone.factor_ref) | copy-start | bytes 24580
  86.5 11.6 %copy-start.15 = (s32[320]{0:T(512)S(1)}, s32[320]{0:T(512)}, u32[]{:S(2)}) copy-start(s32[320]{0:T(512)} %param.19) | copy-start | bytes 3844
  86.5 11.6 %copy-start.16 = (s32[128]{0:T(128)S(1)}, s32[128]{0:T(128)}, u32[]{:S(2)}) copy-start(s32[128]{0:T(128)} %constant.42) | copy-start | bytes 1540
  86.5 78.8 %copy-start.13 = (f32[32,256]{1,0:T(8,128)S(1)}, f32[32,256]{1,0:T(8,128)}, u32[]{:S(2)}) copy-start(f32[32,256]{1,0:T(8,128)} %constant.35.clone.pick_ref) | copy-start | bytes 98308
  176.7 22.5 %copy-start.2 = (f32[2,96,256]{2,1,0:T(8,128)S(1)}, f32[2,96,256]{2,1,0:T(8,128)}, u32[]{:S(2)}) copy-start(f32[2,96,256]{2,1,0:T(8,128)} %constant.29.clone.twist_ref) | copy-start | bytes 589828
  176.8 22.5 %copy-start.3 = (bf16[256,512]{1,0:T(8,128)(2,1)S(1)}, bf16[256,512]{1,0:T(8,128)(2,1)}, u32[]{:S(2)}) copy-start(bf16[256,512]{1,0:T(8,128)(2,1)} %constant.36.clone.back_ref) | copy-start | bytes 786436
  176.8 22.5 %copy-start.6 = (bf16[192,192]{1,0:T(8,128)(2,1)S(1)}, bf16[192,192]{1,0:T(8,128)(2,1)}, u32[]{:S(2)}) copy-start(bf16[192,192]{1,0:T(8,128)(2,1)} %constant.38.clone.ll_ref) | copy-start | bytes 221188
  176.8 22.5 %copy-start.7 = (bf16[192,192]{1,0:T(8,128)(2,1)S(1)}, bf16[192,192]{1,0:T(8,128)(2,1)}, u32[]{:S(2)}) copy-start(bf16[192,192]{1,0:T(8,128)(2,1)} %constant.37.clone.lh_ref) | copy-start | bytes 221188
  176.8 22.5 %copy-start.11 = (s32[5120]{0:T(1024)S(1)}, s32[5120]{0:T(1024)}, u32[]{:S(2)}) copy-start(s32[5120]{0:T(1024)} %slot_ref.3) | copy-start | bytes 61444
Sparse Core Ops, SparseCore 0:
  98.2 65.9 all-reduce.2

commit v2 on v1

--- a/solution.py
+++ b/solution.py
@@ -200,72 +200,184 @@
     )(slots, heights, *t["first"], t["twist"], *t["second"])
 
 
-def analysis_kernel(msg_ref, panel_ref, diag_ref, factor_ref, out_ref):
-    step = pl.program_id(0)
-    for pair in range(2):
-        accs = [None, None]
-        for R in range(16):
-            both = msg_ref[pl.ds(pl.multiple_of(R * 160 + step * 32 + pair * 16, 16), 16), :]
-            both = both.astype(F32)
+MESH = pl.DeviceIdType.MESH
+ROWS_IN = 160
+ROWS_OUT = 48
+SLAB = 80
+
+
+def middle_kernel(msg_ref, panel_ref, keep_ref, diag_ref, factor_ref, pick_ref, out_ref,
+                  pan, got, acc, mine, parts, coeff, syn,
+                  psem, s1, r1, s2, r2, s3, r3, s4, r4):
+    lat = lax.axis_index("lat")
+    me = lax.axis_index("ord")
+    hy, hz, hc = me // 8, me // 2 % 4, me % 2
+
+    def ahead(d):
+        return (hy + d // 8) % 2 * 8 + (hz + d // 2 % 4) % 4 * 2 + (hc + d % 2) % 2
+
+    def behind(d):
+        return (hy + 2 - d // 8) % 2 * 8 + (hz + 4 - d // 2 % 4) % 4 * 2 + (hc + 2 - d % 2) % 2
+
+    def panel_copy(d):
+        place = pl.ds(pl.multiple_of(behind(d) * 16, 16), 16)
+        return pltpu.make_async_copy(panel_ref.at[place], pan.at[place], psem.at[d])
+
+    def in_copy(d):
+        return pltpu.make_async_remote_copy(
+            src_ref=msg_ref.at[pl.ds(pl.multiple_of(ahead(d) * ROWS_IN, 16), ROWS_IN)],
+            dst_ref=got.at[pl.ds(pl.multiple_of(me * ROWS_IN, 16), ROWS_IN)],
+            send_sem=s1.at[d], recv_sem=r1.at[d],
+            device_id=(lat, ahead(d)), device_id_type=MESH,
+        )
+
+    def slab_copy(d):
+        peer = (lat + d) % 8
+        return pltpu.make_async_remote_copy(
+            src_ref=mine.at[pl.ds(pl.multiple_of(peer * SLAB, 16), SLAB)],
+            dst_ref=parts.at[pl.ds(pl.multiple_of(lat * SLAB, 16), SLAB)],
+            send_sem=s2.at[d], recv_sem=r2.at[d],
+            device_id=(peer, me), device_id_type=MESH,
+        )
+
+    def coeff_copy(d):
+        peer = (lat + d) % 8
+        place = pl.ds(pl.multiple_of(lat * SLAB, 16), SLAB)
+        return pltpu.make_async_remote_copy(
+            src_ref=coeff.at[place], dst_ref=coeff.at[place],
+            send_sem=s3.at[d], recv_sem=r3.at[d],
+            device_id=(peer, me), device_id_type=MESH,
+        )
+
+    def out_copy(d):
+        return pltpu.make_async_remote_copy(
+            src_ref=syn.at[pl.ds(pl.multiple_of(ahead(d) * ROWS_OUT, 16), ROWS_OUT)],
+            dst_ref=out_ref.at[pl.ds(pl.multiple_of(me * ROWS_OUT, 16), ROWS_OUT)],
+            send_sem=s4.at[d], recv_sem=r4.at[d],
+            device_id=(lat, ahead(d)), device_id_type=MESH,
+        )
+
+    def loop(low, high, body):
+        def step(d, carry):
+            body(d)
+            return carry
+        lax.fori_loop(low, high, step, 0)
+
+    loop(0, 16, lambda d: panel_copy(d).start())
+    barrier = pltpu.get_barrier_semaphore()
+    loop(1, 16, lambda d: pl.semaphore_signal(barrier, inc=1, device_id=(lat, ahead(d)), device_id_type=MESH))
+    loop(1, 8, lambda d: pl.semaphore_signal(barrier, inc=1, device_id=((lat + d) % 8, me), device_id_type=MESH))
+    pl.semaphore_wait(barrier, 22)
+    loop(1, 16, lambda d: in_copy(d).start())
+
+    def analyse(ref, peer, fresh):
+        def pair(i):
+            both = ref[pl.ds(pl.multiple_of(peer * ROWS_IN + i * 16, 16), 16), :].astype(F32)
             for e in range(2):
                 one = both[e * 8 : e * 8 + 8]
                 two = jnp.concatenate([one, one], 0).astype(BF16)
                 left = jnp.concatenate([two] * 8, 0) * diag_ref[...]
-                g = pair * 2 + e
-                right = panel_ref[R * 16 : R * 16 + 16, g * 16 : g * 16 + 16, :].reshape(256, DEG)
+                right = pan[
+                    pl.ds(pl.multiple_of(peer * 16, 16), 16),
+                    pl.ds(pl.multiple_of(i * 32 + e * 16, 16), 16), :
+                ].reshape(256, DEG)
+                place = pl.ds(pl.multiple_of(i * 256 + e * 128, 128), 128)
                 d = dot(left, right)
-                accs[e] = d if accs[e] is None else accs[e] + d
-        for e in range(2):
-            g = pair * 2 + e
-            acc = accs[e].reshape(16, 8, DEG)
-            for c in range(2):
-                out_ref[c, g * 16 : g * 16 + 16, :] = jnp.sum(acc * factor_ref[c][None], axis=1)
-
-
-def analysis(msg, panels, factors):
+                acc[place, :] = d if fresh else acc[place, :] + d
+        loop(0, 10, pair)
+
+    panel_copy(0).wait()
+    analyse(msg_ref, me, True)
+
+    def arrived(d):
+        in_copy(d).wait_recv()
+        panel_copy(d).wait()
+        analyse(got, behind(d), False)
+
+    loop(1, 16, arrived)
+
+    def fold(g):
+        rows = acc[pl.ds(pl.multiple_of(g * 128, 128), 128), :].reshape(16, 8, DEG)
+        for c in range(2):
+            mine[pl.ds(pl.multiple_of(c * 320 + g * 16, 16), 16), :] = jnp.sum(
+                rows * factor_ref[c][None], axis=1
+            )
+
+    loop(0, 20, fold)
+    loop(1, 8, lambda d: slab_copy(d).start())
+    own = pl.ds(pl.multiple_of(lat * SLAB, 16), SLAB)
+    total = mine[own, :]
+    for d in range(1, 8):
+        slab_copy(d).wait_recv()
+        total = total + parts[pl.ds(pl.multiple_of((lat + 8 - d) % 8 * SLAB, 16), SLAB), :]
+    keep = keep_ref[pl.ds(pl.multiple_of(lat % 4 * SLAB, 16), SLAB), :]
+    coeff[own, :] = (total * keep).astype(BF16)
+    loop(1, 8, lambda d: coeff_copy(d).start())
+    loop(1, 8, lambda d: coeff_copy(d).wait_recv())
+
+    def synthesise(ref, peer, row):
+        def four(i):
+            outs = []
+            for e in range(8):
+                g = jnp.minimum(i * 8 + e, 19)
+                left = jnp.concatenate(
+                    [coeff[pl.ds(pl.multiple_of(c * 320 + g * 16, 16), 16), :] for c in range(2)], 0
+                )
+                right = pan[
+                    pl.ds(pl.multiple_of(peer * 16, 16), 16), pl.ds(pl.multiple_of(g * 16, 16), 16), :
+                ].reshape(256, DEG)
+                d = lax.dot_general(left, right, (((1,), (1,)), ((), ())), preferred_element_type=F32)
+                d = d * pick_ref[...]
+                for c in range(2):
+                    outs.append(jnp.sum(d[c * 16 : c * 16 + 16], axis=0, keepdims=True))
+            ref[pl.ds(pl.multiple_of(row * ROWS_OUT + i * 16, 16), 16), :] = jnp.concatenate(outs, 0).astype(BF16)
+        loop(0, 3, four)
+
+    def leaving(i):
+        d = 16 - i
+        synthesise(syn, ahead(d), ahead(d))
+        out_copy(d).start()
+
+    loop(1, 16, leaving)
+    synthesise(out_ref, me, me)
+
+    def finish(d):
+        in_copy(d).wait_send()
+        out_copy(d).wait()
+
+    loop(1, 16, finish)
+
+    def finish_lat(d):
+        slab_copy(d).wait_send()
+        coeff_copy(d).wait_send()
+
+    loop(1, 8, finish_lat)
+
+
+def middle(msg, panels, keep, factors):
     t = tables()
+    dma = pltpu.SemaphoreType.DMA
     return pl.pallas_call(
-        analysis_kernel,
-        grid=(5,),
-        out_shape=jax.ShapeDtypeStruct((2, 320, DEG), F32),
-        in_specs=[
-            pl.BlockSpec((ORDERS // 2, 256), lambda i: (0, 0)),
-            pl.BlockSpec((256, 64, DEG), lambda i: (0, i, 0)),
-            pl.BlockSpec((128, 256), lambda i: (0, 0)),
-            pl.BlockSpec((2, 8, DEG), lambda i: (0, 0, 0)),
+        middle_kernel,
+        out_shape=jax.ShapeDtypeStruct((16 * ROWS_OUT, 256), BF16),
+        in_specs=[vmem(), pl.BlockSpec(memory_space=pl.ANY)] + [vmem()] * 4,
+        out_specs=vmem(),
+        scratch_shapes=[
+            pltpu.VMEM((256, 320, DEG), BF16),
+            pltpu.VMEM((16 * ROWS_IN, 256), BF16),
+            pltpu.VMEM((20 * 128, DEG), F32),
+            pltpu.VMEM((640, DEG), F32),
+            pltpu.VMEM((640, DEG), F32),
+            pltpu.VMEM((640, DEG), BF16),
+            pltpu.VMEM((16 * ROWS_OUT, 256), BF16),
+            dma((16,)), dma((16,)), dma((16,)), dma((8,)), dma((8,)), dma((8,)), dma((8,)), dma((16,)), dma((16,)),
         ],
-        out_specs=pl.BlockSpec((2, 64, DEG), lambda i: (0, i, 0)),
-        compiler_params=pltpu.CompilerParams(vmem_limit_bytes=48 * MIB),
-        name="analysis",
-    )(msg, panels, t["diag"], factors)
-
-
-def synthesis_kernel(coeff_ref, panel_ref, pick_ref, out_ref):
-    for g in range(4):
-        left = jnp.concatenate([coeff_ref[c, g * 16 : g * 16 + 16, :] for c in range(2)], 0)
-        for R in range(16):
-            right = panel_ref[R * 16 : R * 16 + 16, g * 16 : g * 16 + 16, :].reshape(256, DEG)
-            d = lax.dot_general(left, right, (((1,), (1,)), ((), ())), preferred_element_type=F32)
-            d = d * pick_ref[...]
-            out_ref[R, g * 2 : g * 2 + 1, :] = jnp.sum(d[:16], axis=0, keepdims=True)
-            out_ref[R, g * 2 + 1 : g * 2 + 2, :] = jnp.sum(d[16:], axis=0, keepdims=True)
-
-
-def synthesize(coeffs, panels):
-    t = tables()
-    return pl.pallas_call(
-        synthesis_kernel,
-        grid=(5,),
-        out_shape=jax.ShapeDtypeStruct((16, 40, 256), F32),
-        in_specs=[
-            pl.BlockSpec((2, 64, DEG), lambda i: (0, i, 0)),
-            pl.BlockSpec((256, 64, DEG), lambda i: (0, i, 0)),
-            pl.BlockSpec((32, 256), lambda i: (0, 0)),
-        ],
-        out_specs=pl.BlockSpec((16, 8, 256), lambda i: (0, i, 0)),
-        compiler_params=pltpu.CompilerParams(vmem_limit_bytes=48 * MIB),
-        name="synthesis",
-    )(coeffs, panels, t["pick"])
+        compiler_params=pltpu.CompilerParams(
+            vmem_limit_bytes=48 * MIB, collective_id=0, has_side_effects=True
+        ),
+        cost_estimate=pl.CostEstimate(flops=8 * 10**9, bytes_accessed=24 * 10**6, transcendentals=0),
+        name="middle",
+    )(msg, panels, keep, t["diag"], factors, t["pick"])
 
 
 def inverse_kernel(slot_ref, msg_ref, back_ref, twist_ref, lh_ref, ll_ref, out_ref, ts, ls, ys):
@@ -358,13 +470,8 @@
 
 def local(heights, panels, ord_slot, cutoffs):
     msg = forward(heights, ord_slot)
-    got = lax.all_to_all(msg, "ord", split_axis=0, concat_axis=0, tiled=True)
-    folded = lax.psum(analysis(got, panels, factor_rows()), "lat")
     keep = (degrees()[None, :] <= cutoffs[:, None]).astype(F32)
-    coeffs = (folded * keep[None]).astype(BF16)
-    synth = synthesize(coeffs, panels)
-    synth = jnp.pad(synth.astype(BF16), ((0, 0), (0, 8), (0, 0))).reshape(16 * 48, 256)
-    back = lax.all_to_all(synth, "ord", split_axis=0, concat_axis=0, tiled=True)
+    back = middle(msg, panels, keep, factor_rows())
     return inverse(back, ord_slot)
 
 

time: 240 us -> 159 us (0.66)
  waiting for transfers between devices: 66 us -> 0 us
  blocking collectives: 51.6 us -> 0 us
  Pallas kernels: 99.9 us -> 151 us
  between operations: 13.6 us -> 0.14 us
    psum x1 -> x0, waiting for transfers between devices: 66 us -> none  [local(): folded = lax.psum(analysis(got, panels, factor_rows()), 'lat')]
    all_to_all x2 -> x0, blocking collectives: 51.6 us -> none  [the longest x1 29.3 us: local(): got = lax.all_to_all(msg, 'ord', split_axis=0, concat_axis=0, tiled=True)]
    pallas_call x2 -> x1, Pallas kernels: 23 us -> 74.2 us  [middle(): pl.pallas_call(middle_kernel, out_shape=jax.ShapeDtypeStruct((16 * ROWS_O...]
    unnamed x34 -> x28, local copies, waits for them, and re-layouts: 6.74 us -> 6.71 us
  transfers between devices with their start and end apart: 1 -> 0, of which waited for: 1 -> 0; matrix products, arithmetic and copies ran while one was open for 0% -> 0% of each run, Pallas kernels for 0% -> 0%
where the time goes in v2:
time: 159 us
  Pallas kernels  151 us (95%)
  local copies, waits for them, and re-layouts  6.71 us (4%)
    pallas_call x1, Pallas kernels, middle(): pl.pallas_call(middle_kernel, out_shape=jax.ShapeDtypeStruct((16 * ROWS_O...  74.2 us
    pallas_call x1, Pallas kernels, forward(): pl.pallas_call(forward_kernel, out_shape=jax.ShapeDtypeStruct((ORDERS //...  43.7 us
    pallas_call x1, Pallas kernels, inverse(): pl.pallas_call(inverse_kernel, out_shape=jax.ShapeDtypeStruct((CYC, LON),...  33 us
    unnamed x28, local copies, waits for them, and re-layouts  6.71 us

profile of v2, /device:TPU:1, one launch (start us, length us, event | category | flops | bytes accessed | tf_op | source)
XLA Modules:
  0.0 158.6 jit_solution(13806352374100481635)
XLA Ops:
  0.0 0.0 copy-start.12
  0.0 0.0 copy-start.13
  0.0 0.0 copy-start.11
  0.0 0.8 compare_convert_fusion.keep_ref
  0.9 0.0 copy-start
  0.9 1.3 copy-done
  2.2 0.0 copy-start.1
  2.2 0.9 copy-done.1
  3.1 0.0 copy-start.4
  3.1 0.9 copy-done.4
  4.1 0.0 copy-start.5
  4.1 0.9 copy-done.5
  5.0 0.0 copy-start.8
  5.0 0.9 copy-done.8
  5.9 0.0 copy-start.9
  5.9 0.9 copy-done.9
  6.8 0.0 copy-start.10
  6.8 0.7 copy-done.10
  7.5 43.7 %forward.1.msg_ref = bf16[2560,256]{1,0:T(8,128)(2,1)S(1)} custom-call(s32[5120]{0:T(1024)S(1)} %copy-done.10, bf16[16,43200]{1,0:T(8,128)(2,1)S(1)} %copy-done, bf16[192,192]{1,0:T(8,128)(2,1)S(1)} %copy-done.9, bf16[192,192]{1,0:T(8,128)(2,1)S(1)} %copy-done.8, f32[2,96,256]{2,1,0:T(8,128)S(1)} %copy-done.1, bf16[512,256]{1,0:T(8,128)(2,1)S(1)} %copy-done.5, ...), custom_call_target="tpu_custom_call" | custom-call | tf_op jit(solution)/shard_map/forward/pallas_call | solution.py:187
  51.3 0.0 copy-done.12
  51.3 0.0 copy-done.13
  51.3 0.0 copy-done.11
  51.3 0.0 copy-start.2
  51.3 0.0 copy-start.3
  51.3 0.0 copy-start.6
  51.4 0.0 copy-start.7
  51.4 74.2 %middle.1.msg_ref = bf16[768,256]{1,0:T(8,128)(2,1)S(1)} custom-call(bf16[2560,256]{1,0:T(8,128)(2,1)S(1)} %forward.1.msg_ref, bf16[256,320,128]{2,1,0:T(8,128)(2,1)} %panel_ref.1, f32[320,128]{1,0:T(8,128)S(1)} %compare_convert_fusion.keep_ref, bf16[128,256]{1,0:T(8,128)(2,1)S(1)} %copy-done.11, f32[2,8,128]{2,1,0:T(8,128)S(1)} %copy-done.13, ...), custom_call_target="tpu_custom_call" | custom-call | flops 8000000000 | bytes 24000000 | tf_op jit(solution)/shard_map/middle/pallas_call | solution.py:360
  125.5 0.0 copy-done.2
  125.5 0.0 copy-done.3
  125.6 0.0 copy-done.6
  125.6 0.0 copy-done.7
  125.6 33.0 %inverse.1 = f32[16,43200]{1,0:T(8,128)} custom-call(s32[5120]{0:T(1024)S(1)} %copy-done.10, bf16[768,256]{1,0:T(8,128)(2,1)S(1)} %middle.1.msg_ref, bf16[256,512]{1,0:T(8,128)(2,1)S(1)} %copy-done.3, f32[2,96,256]{2,1,0:T(8,128)S(1)} %copy-done.2, bf16[192,192]{1,0:T(8,128)(2,1)S(1)} %copy-done.7, bf16[192,192]{1,0:T(8,128)(2,1)S(1)} %copy-done.6), custom_call_target="tpu_custom_call" | custom-call | tf_op jit(solution)/shard_map/inverse/pallas_call | solution.py:441
Async XLA Ops:
  0.0 51.3 %copy-start.12 = (f32[32,256]{1,0:T(8,128)S(1)}, f32[32,256]{1,0:T(8,128)}, u32[]{:S(2)}) copy-start(f32[32,256]{1,0:T(8,128)} %constant.32.clone.pick_ref) | copy-start | bytes 98308
  0.0 51.3 %copy-start.13 = (f32[2,8,128]{2,1,0:T(8,128)S(1)}, f32[2,8,128]{2,1,0:T(8,128)}, u32[]{:S(2)}) copy-start(f32[2,8,128]{2,1,0:T(8,128)} %constant.31.clone.factor_ref) | copy-start | bytes 24580
  0.0 51.3 %copy-start.11 = (bf16[128,256]{1,0:T(8,128)(2,1)S(1)}, bf16[128,256]{1,0:T(8,128)(2,1)}, u32[]{:S(2)}) copy-start(bf16[128,256]{1,0:T(8,128)(2,1)} %constant.30.clone.diag_ref) | copy-start | bytes 196612
  0.9 1.3 copy-start
  2.2 0.9 copy-start.1
  3.1 0.9 copy-start.4
  4.1 0.9 copy-start.5
  5.0 0.9 copy-start.8
  5.9 0.9 copy-start.9
  6.8 0.7 copy-start.10
  51.3 74.2 %copy-start.2 = (f32[2,96,256]{2,1,0:T(8,128)S(1)}, f32[2,96,256]{2,1,0:T(8,128)}, u32[]{:S(2)}) copy-start(f32[2,96,256]{2,1,0:T(8,128)} %constant.26.clone.twist_ref) | copy-start | bytes 589828
  51.3 74.2 %copy-start.3 = (bf16[256,512]{1,0:T(8,128)(2,1)S(1)}, bf16[256,512]{1,0:T(8,128)(2,1)}, u32[]{:S(2)}) copy-start(bf16[256,512]{1,0:T(8,128)(2,1)} %constant.33.clone.back_ref) | copy-start | bytes 786436
  51.3 74.2 %copy-start.6 = (bf16[192,192]{1,0:T(8,128)(2,1)S(1)}, bf16[192,192]{1,0:T(8,128)(2,1)}, u32[]{:S(2)}) copy-start(bf16[192,192]{1,0:T(8,128)(2,1)} %constant.35.clone.ll_ref) | copy-start | bytes 221188
  51.4 74.2 %copy-start.7 = (bf16[192,192]{1,0:T(8,128)(2,1)S(1)}, bf16[192,192]{1,0:T(8,128)(2,1)}, u32[]{:S(2)}) copy-start(bf16[192,192]{1,0:T(8,128)(2,1)} %constant.34.clone.lh_ref) | copy-start | bytes 221188

commit v3 on v2

v3 whole, which is shorter than its diff:
```python
import functools
import math

import jax
import jax.numpy as jnp
import numpy as np
from jax import lax
from jax.experimental import pallas as pl
from jax.experimental.pallas import tpu as pltpu
from jax.sharding import PartitionSpec as P

LON = 43200
SLOW = 180
FAST = 240
HALF = 96
ORDERS = 5120
DEG = 128
NMAX = 21600
CYC = 16
TROWS = 6016
F32 = jnp.float32
BF16 = jnp.bfloat16
MIB = 1024 * 1024


def split16(table):
    high = table.astype(np.float32).astype(jnp.bfloat16)
    low = (table - high.astype(np.float64)).astype(np.float32).astype(jnp.bfloat16)
    return high, low


def angles(left, right, total):
    return 2.0 * np.pi / total * ((left[:, None] * right[None, :]) % total)


@functools.cache
def tables():
    k = np.arange(91)
    a = np.arange(SLOW)
    b = np.arange(FAST)
    q = np.arange(29)
    ka = angles(k, a, SLOW)
    first = np.zeros((2, HALF, 192))
    first[0, :91, :SLOW] = np.cos(ka)
    first[1, :91, :SLOW] = -np.sin(ka)
    first = first.reshape(2 * HALF, 192)
    kb = angles(k, b, LON)
    twist = np.zeros((2, HALF, 256), np.float32)
    twist[0, :91, :FAST] = np.cos(kb)
    twist[1, :91, :FAST] = np.sin(kb)
    bq = angles(b, q, FAST)
    bq1 = angles(b, q + 1, FAST)
    second = np.zeros((2, 256, 2, 128))
    second[0, :FAST, 0, 0:29] = np.cos(bq)
    second[1, :FAST, 0, 0:29] = np.sin(bq)
    second[0, :FAST, 1, 0:29] = -np.sin(bq)
    second[1, :FAST, 1, 0:29] = np.cos(bq)
    second[0, :FAST, 0, 32:61] = np.cos(bq1)
    second[1, :FAST, 0, 32:61] = -np.sin(bq1)
    second[0, :FAST, 1, 32:61] = -np.sin(bq1)
    second[1, :FAST, 1, 32:61] = -np.cos(bq1)
    second[..., 64:] = second[..., :64]
    second = second.reshape(512, 256) / math.sqrt(LON)
    back = np.zeros((2, 2, 32, 2, 256))
    back[0, 0, :29, 0, :FAST] = np.cos(bq).T
    back[0, 0, :29, 1, :FAST] = np.sin(bq).T
    back[1, 0, :29, 0, :FAST] = -np.sin(bq).T
    back[1, 0, :29, 1, :FAST] = np.cos(bq).T
    back[0, 1, :29, 0, :FAST] = np.cos(bq1).T
    back[0, 1, :29, 1, :FAST] = -np.sin(bq1).T
    back[1, 1, :29, 0, :FAST] = -np.sin(bq1).T
    back[1, 1, :29, 1, :FAST] = -np.cos(bq1).T
    back = np.concatenate(split16(back.reshape(128, 512)), 0)
    last = np.zeros((192, 2, HALF))
    last[:SLOW, 0, :91] = np.cos(ka).T
    last[:SLOW, 1, :91] = -np.sin(ka).T
    last = last.reshape(192, 2 * HALF) * math.sqrt(2048 / (DEG * ORDERS))
    rows = np.arange(128)
    lanes = np.arange(256)
    diag = (lanes[None, :] % 16 == rows[:, None] // 8).astype(jnp.bfloat16)
    pick = (lanes[None, :] % 16 == np.arange(32)[:, None] % 16).astype(np.float32)
    return dict(
        first=split16(first), twist=twist, second=split16(second), back=back,
        last=split16(last), diag=diag, pick=pick,
    )


def swap_chunks(rows):
    rows = list(rows)
    chunk = lax.broadcasted_iota(jnp.int32, (8, 128), 1) // 16
    for d in (4, 2, 1):
        low = (chunk & d) == 0
        new = list(rows)
        for r in range(8):
            if r & d:
                continue
            new[r] = jnp.where(low, rows[r], pltpu.roll(rows[r + d], d * 16, 1))
            new[r + d] = jnp.where(low, pltpu.roll(rows[r], 128 - d * 16, 1), rows[r + d])
        rows = new
    return rows


def dot(left, right):
    return jnp.dot(left, right, preferred_element_type=F32)


def halves(value):
    high = value.astype(BF16)
    return high, (value - high.astype(F32)).astype(BF16)


def vmem():
    return pl.BlockSpec(memory_space=pltpu.VMEM)


MESH = pl.DeviceIdType.MESH
ROWS_IN = 160
ROWS_OUT = 48
SLAB = 80


def main_kernel(slot_ref, x_hbm, fh_hbm, fl_hbm, twist_hbm, sh_hbm, sl_hbm, panel_ref, keep_ref, diag_ref,
                factor_ref, pick_ref, out_ref,
                x_ref, fh_ref, fl_ref, twist_ref, sh_ref, sl_ref, xs, qs, ts, gs, msg_ref,
                pan, got, mine, parts, coeff, syn,
                xsem, tsem, psem, s1, r1, s2, r2, s3, r3, s4, r4):
    lat = lax.axis_index("lat")
    me = lax.axis_index("ord")
    hy, hz, hc = me // 8, me // 2 % 4, me % 2

    def ahead(d):
        return (hy + d // 8) % 2 * 8 + (hz + d // 2 % 4) % 4 * 2 + (hc + d % 2) % 2

    def behind(d):
        return (hy + 2 - d // 8) % 2 * 8 + (hz + 4 - d // 2 % 4) % 4 * 2 + (hc + 2 - d % 2) % 2

    def panel_copy(d):
        place = pl.ds(pl.multiple_of(behind(d) * 16, 16), 16)
        return pltpu.make_async_copy(panel_ref.at[place], pan.at[place], psem.at[d])

    def in_copy(d):
        return pltpu.make_async_remote_copy(
            src_ref=msg_ref.at[pl.ds(pl.multiple_of(ahead(d) * ROWS_IN, 16), ROWS_IN)],
            dst_ref=got.at[pl.ds(pl.multiple_of(me * ROWS_IN, 16), ROWS_IN)],
            send_sem=s1.at[d], recv_sem=r1.at[d],
            device_id=(lat, ahead(d)), device_id_type=MESH,
        )

    def slab_copy(d):
        peer = (lat + d) % 8
        return pltpu.make_async_remote_copy(
            src_ref=mine.at[pl.ds(pl.multiple_of(peer * SLAB, 16), SLAB)],
            dst_ref=parts.at[pl.ds(pl.multiple_of(lat * SLAB, 16), SLAB)],
            send_sem=s2.at[d], recv_sem=r2.at[d],
            device_id=(peer, me), device_id_type=MESH,
        )

    def coeff_copy(d):
        peer = (lat + d) % 8
        place = pl.ds(pl.multiple_of(lat * SLAB, 16), SLAB)
        return pltpu.make_async_remote_copy(
            src_ref=coeff.at[place], dst_ref=coeff.at[place],
            send_sem=s3.at[d], recv_sem=r3.at[d],
            device_id=(peer, me), device_id_type=MESH,
        )

    def out_copy(d):
        return pltpu.make_async_remote_copy(
            src_ref=syn.at[pl.ds(pl.multiple_of(ahead(d) * ROWS_OUT, 16), ROWS_OUT)],
            dst_ref=out_ref.at[pl.ds(pl.multiple_of(me * ROWS_OUT, 16), ROWS_OUT)],
            send_sem=s4.at[d], recv_sem=r4.at[d],
            device_id=(lat, ahead(d)), device_id_type=MESH,
        )

    def loop(low, high, body):
        def step(d, carry):
            body(d)
            return carry
        lax.fori_loop(low, high, step, 0)

    heights_copy = pltpu.make_async_copy(x_hbm, x_ref, xsem)
    heights_copy.start()
    held = ((fh_hbm, fh_ref), (fl_hbm, fl_ref), (twist_hbm, twist_ref), (sh_hbm, sh_ref), (sl_hbm, sl_ref))

    def table_copy(i):
        return pltpu.make_async_copy(held[i][0], held[i][1], tsem.at[i])

    for i in range(5):
        table_copy(i).start()
    loop(0, 16, lambda d: panel_copy(d).start())
    barrier = pltpu.get_barrier_semaphore()
    loop(1, 16, lambda d: pl.semaphore_signal(barrier, inc=1, device_id=(lat, ahead(d)), device_id_type=MESH))
    loop(1, 8, lambda d: pl.semaphore_signal(barrier, inc=1, device_id=((lat + d) % 8, me), device_id_type=MESH))
    heights_copy.wait()
    inside = lax.broadcasted_iota(jnp.int32, (CYC, 256), 1) < FAST
    for r in range(CYC):
        for lane in range(2):
            xs[lane, r * 192 + 176 : r * 192 + 192, :] = jnp.zeros((16, 128), F32)
    for a in range(SLOW):
        start = FAST * a // 128 * 128
        off = FAST * a - start
        if start + 384 <= LON:
            v = x_ref[:, start : start + 384].astype(F32)
        else:
            v = jnp.concatenate(
                [x_ref[:, start:LON].astype(F32), jnp.zeros((CYC, start + 384 - LON), F32)], 1
            )
        if off:
            v = pltpu.roll(v, 384 - off, 1)
        v = jnp.where(inside, v[:, :256], 0.0)
        for lane in range(2):
            xs.at[lane][pl.ds(a, CYC, stride=192), :] = v[:, lane * 128 : lane * 128 + 128]

    first = lax.broadcasted_iota(jnp.int32, (48, 128), 1) < 64

    def one_cycle(r, carry):
        rows = pl.ds(pl.multiple_of(r * 192, 192), 192)
        level = jnp.concatenate([xs[0, rows, :], xs[1, rows, :]], 1)
        value = level
        for p in range(3):
            if p:
                value = value * level
            if p == 0:
                high = value.astype(BF16)
                y = dot(fh_ref[...], high) + dot(fl_ref[...], high)
            else:
                high, low = halves(value)
                y = dot(fh_ref[...], high) + dot(fl_ref[...], high) + dot(fh_ref[...], low)
            re, im = y[:HALF], y[HALF:]
            tc, tsin = twist_ref[0], twist_ref[1]
            z = jnp.concatenate([re * tc + im * tsin, im * tc - re * tsin], 1)
            zh, zl = halves(z)
            o = dot(zh, sh_ref[...]) + dot(zh, sl_ref[...]) + dot(zl, sh_ref[...])
            for c in range(2):
                part = o[:, c * 128 : c * 128 + 128]
                qs[pl.ds(r * 8 + c * 3 + p, 48, stride=128), :] = jnp.where(first, part[:48], part[48:])
        for x in (6, 7):
            qs[pl.ds(r * 8 + x, 48, stride=128), :] = jnp.zeros((48, 128), F32)
        return carry

    for i in range(5):
        table_copy(i).wait()
    lax.fori_loop(0, CYC, one_cycle, 0)

    def one_k(k, carry):
        t = qs[pl.ds(pl.multiple_of(k * 128, 128), 128), :].T
        ts[pl.ds(k, 32, stride=SLOW), :] = t[0:32]
        ts[pl.ds(SLOW - k, 32, stride=SLOW), :] = t[32:64]
        return t

    def two_k(k, carry):
        t = one_k(k, carry)
        ts[pl.ds(k + 48, 32, stride=SLOW), :] = t[64:96]
        ts[pl.ds(SLOW - 48 - k, 32, stride=SLOW), :] = t[96:128]
        return carry

    def only_k(k, carry):
        one_k(k, carry)
        return carry

    lax.fori_loop(0, 43, two_k, 0)
    lax.fori_loop(43, 48, only_k, 0)

    pl.semaphore_wait(barrier, 22)

    def one_chip(i, carry):
        far = 7 - i
        chip = (hy + far // 4) % 2 * 4 + (hz + far % 4) % 4
        for j in range(5):
            tile = chip * 5 + j
            for i in range(0, 128, 32):
                rows = [ts[pl.ds(slot_ref[tile * 128 + i + e] + 1, 1), :] for e in range(32)]
                for e in range(32):
                    gs[j, i + e : i + e + 1, :] = rows[e]
            t = gs[j].T
            sides = []
            for h in range(2):
                sides.append(
                    jnp.concatenate(swap_chunks([t[(h * 8 + r) * 8 : (h * 8 + r + 1) * 8] for r in range(8)]), 0)
                )
            msg_ref[pl.ds(pl.multiple_of(tile * 64, 64), 64), :] = jnp.concatenate(sides, 1).astype(BF16)

        @pl.when(far > 0)
        def _():
            in_copy(far * 2).start()

        in_copy(far * 2 + 1).start()
        return carry

    lax.fori_loop(0, 8, one_chip, 0)
    own_in = pl.ds(pl.multiple_of(me * ROWS_IN, 16), ROWS_IN)
    got[own_in, :] = msg_ref[own_in, :]
    loop(0, 16, lambda d: panel_copy(d).wait())
    loop(1, 16, lambda d: in_copy(d).wait_recv())

    def analyse(i):
        accs = [None, None]
        for R in range(16):
            both = got[pl.ds(pl.multiple_of(R * ROWS_IN + i * 16, 16), 16), :].astype(F32)
            for e in range(2):
                one = both[e * 8 : e * 8 + 8]
                two = jnp.concatenate([one, one], 0).astype(BF16)
                left = jnp.concatenate([two] * 8, 0) * diag_ref[...]
                right = pan[
                    R * 16 : R * 16 + 16, pl.ds(pl.multiple_of(i * 32 + e * 16, 16), 16), :
                ].reshape(256, DEG)
                d = dot(left, right)
                accs[e] = d if R == 0 else accs[e] + d
        for e in range(2):
            rows = accs[e].reshape(16, 8, DEG)
            for c in range(2):
                mine[pl.ds(pl.multiple_of(c * 320 + i * 32 + e * 16, 16), 16), :] = jnp.sum(
                    rows * factor_ref[c][None], axis=1
                )

    loop(0, 10, analyse)
    loop(1, 8, lambda d: slab_copy(d).start())
    own = pl.ds(pl.multiple_of(lat * SLAB, 16), SLAB)
    total = mine[own, :]
    for d in range(1, 8):
        slab_copy(d).wait_recv()
        total = total + parts[pl.ds(pl.multiple_of((lat + 8 - d) % 8 * SLAB, 16), SLAB), :]
    keep = keep_ref[pl.ds(pl.multiple_of(lat % 4 * SLAB, 16), SLAB), :]
    coeff[own, :] = (total * keep).astype(BF16)
    loop(1, 8, lambda d: coeff_copy(d).start())
    loop(1, 8, lambda d: coeff_copy(d).wait_recv())

    def synthesise(ref, peer, row):
        def four(i):
            outs = []
            for e in range(8):
                g = jnp.minimum(i * 8 + e, 19)
                left = jnp.concatenate(
                    [coeff[pl.ds(pl.multiple_of(c * 320 + g * 16, 16), 16), :] for c in range(2)], 0
                )
                right = pan[
                    pl.ds(pl.multiple_of(peer * 16, 16), 16), pl.ds(pl.multiple_of(g * 16, 16), 16), :
                ].reshape(256, DEG)
                d = lax.dot_general(left, right, (((1,), (1,)), ((), ())), preferred_element_type=F32)
                d = d * pick_ref[...]
                for c in range(2):
                    outs.append(jnp.sum(d[c * 16 : c * 16 + 16], axis=0, keepdims=True))
            ref[pl.ds(pl.multiple_of(row * ROWS_OUT + i * 16, 16), 16), :] = jnp.concatenate(outs, 0).astype(BF16)
        loop(0, 3, four)

    def leaving(i):
        d = 16 - i
        synthesise(syn, ahead(d), ahead(d))
        out_copy(d).start()

    loop(1, 16, leaving)
    synthesise(out_ref, me, me)

    def finish(d):
        in_copy(d).wait_send()
        out_copy(d).wait()

    loop(1, 16, finish)

    def finish_lat(d):
        slab_copy(d).wait_send()
        coeff_copy(d).wait_send()

    loop(1, 8, finish_lat)


def main(heights, slots, panels, keep, factors):
    t = tables()
    dma = pltpu.SemaphoreType.DMA
    vec = pltpu.VMEM
    hbm = pl.BlockSpec(memory_space=pl.ANY)
    return pl.pallas_call(
        main_kernel,
        out_shape=jax.ShapeDtypeStruct((16 * ROWS_OUT, 256), BF16),
        in_specs=[pl.BlockSpec(memory_space=pltpu.SMEM)] + [hbm] * 7 + [vmem()] * 4,
        out_specs=vmem(),
        scratch_shapes=[
            vec((CYC, LON), BF16),
            vec((192, 192), BF16),
            vec((192, 192), BF16),
            vec((2, HALF, 256), F32),
            vec((512, 256), BF16),
            vec((512, 256), BF16),
            vec((2, CYC * 192, 128), F32),
            vec((48 * 128, 128), F32),
            vec((TROWS, 128), F32),
            vec((5, 128, 128), F32),
            vec((16 * ROWS_IN, 256), BF16),
            vec((256, 320, DEG), BF16),
            vec((16 * ROWS_IN, 256), BF16),
            vec((640, DEG), F32),
            vec((640, DEG), F32),
            vec((640, DEG), BF16),
            vec((16 * ROWS_OUT, 256), BF16),
            dma, dma((5,)), dma((16,)), dma((16,)), dma((16,)), dma((8,)), dma((8,)), dma((8,)), dma((8,)),
            dma((16,)), dma((16,)),
        ],
        compiler_params=pltpu.CompilerParams(
            vmem_limit_bytes=56 * MIB, collective_id=0, has_side_effects=True
        ),
        cost_estimate=pl.CostEstimate(flops=2 * 10**10, bytes_accessed=24 * 10**6, transcendentals=0),
        name="main",
    )(slots, heights, *t["first"], t["twist"], *t["second"], panels, keep, t["diag"], factors, t["pick"])


def inverse_kernel(slot_ref, msg_ref, back_ref, twist_ref, lh_ref, ll_ref, out_ref, ts, ls, ys):
    ts[0:8, :] = jnp.zeros((8, 128), F32)
    ts[ORDERS:TROWS, :] = jnp.zeros((TROWS - ORDERS, 128), F32)

    sub = lax.broadcasted_iota(jnp.int32, (8, 128), 0)

    def one_peer(o, carry):
        for part in range(3):
            rows = msg_ref[pl.ds(pl.multiple_of(o * 48 + part * 16, 16), 16), :].astype(F32)
            count = 128 if part < 2 else 64
            groups = []
            for g in range(8):
                half = rows[g // 4 * 8 : g // 4 * 8 + 8]
                v0, v1 = half[:, :128], half[:, 128:]
                at = g % 4
                v0 = pltpu.roll(v0, 8 - 2 * at, 0) if at else v0
                v1 = pltpu.roll(v1, (10 - 2 * at) % 8, 0) if at != 1 else v1
                groups.append(jnp.where(sub < 2, v0, v1))
            blocks = swap_chunks(groups)
            packed = [jnp.where(sub < 4, blocks[2 * i], pltpu.roll(blocks[2 * i + 1], 4, 0)) for i in range(4)]
            t = jnp.concatenate(packed, 0).T
            base = o * 320 + part * 128
            for i in range(count):
                ts[pl.ds(slot_ref[base + i] + 1, 1), 0:32] = t[i : i + 1]
        return carry

    lax.fori_loop(0, 16, one_peer, 0)

    def one_k(k, carry):
        stack = []
        for base in (0, 48):
            plus = ts[pl.ds(k + base, 32, stride=SLOW), :]
            minus = ts[pl.ds(SLOW - base - k, 32, stride=SLOW), :]
            lone = k == 0 if base == 0 else k == 90 - base
            stack += [plus, jnp.where(lone, 0.0, minus)]
        ls[pl.ds(k, 32, stride=48), :] = jnp.concatenate(stack, 0)[:, :32].T
        return carry

    lax.fori_loop(0, 48, one_k, 0)
    first = lax.broadcasted_iota(jnp.int32, (48, 128), 1) < 64

    def one_cycle(r, carry):
        at = (r % 8 * 4 + r // 8 * 2) * 48
        l0 = ls[pl.ds(pl.multiple_of(at, 48), 48), :]
        l1 = ls[pl.ds(pl.multiple_of(at + 48, 48), 48), :]
        left = jnp.concatenate(
            [jnp.where(first, l0, pltpu.roll(l1, 64, 1)), jnp.where(first, pltpu.roll(l0, 64, 1), l1)], 0
        ).astype(BF16)
        w = dot(jnp.concatenate([left, left], 1), back_ref[...])
        re, im = w[:, :256], w[:, 256:]
        c, s = twist_ref[0], twist_ref[1]
        v = jnp.concatenate([re * c - im * s, im * c + re * s], 0).astype(BF16)
        field = dot(lh_ref[...], v) + dot(ll_ref[...], v)
        for lane in range(2):
            ys[lane, pl.ds(pl.multiple_of(r * 192, 192), 192), :] = field[:, lane * 128 : lane * 128 + 128]
        return carry

    lax.fori_loop(0, CYC, one_cycle, 0, unroll=2)
    for a in range(SLOW):
        v = jnp.concatenate([ys.at[lane][pl.ds(a, CYC, stride=192), :] for lane in range(2)], 1)
        out_ref[:, FAST * a : FAST * a + FAST] = v[:, :FAST]


def inverse(msg, slots):
    t = tables()
    return pl.pallas_call(
        inverse_kernel,
        out_shape=jax.ShapeDtypeStruct((CYC, LON), F32),
        in_specs=[pl.BlockSpec(memory_space=pltpu.SMEM)] + [vmem()] * 5,
        out_specs=vmem(),
        scratch_shapes=[
            pltpu.VMEM((TROWS, 128), F32),
            pltpu.VMEM((32 * 48, 128), F32),
            pltpu.VMEM((2, CYC * 192, 128), F32),
        ],
        compiler_params=pltpu.CompilerParams(vmem_limit_bytes=48 * MIB),
        name="inverse",
    )(slots, msg, t["back"], t["twist"], *t["last"])


def degrees():
    stride = (NMAX - ORDERS) // DEG
    return ORDERS + np.arange(DEG, dtype=np.int32) * stride


def factor_rows():
    degree = degrees().astype(np.float64)
    rows = np.zeros((2, 8, DEG), np.float32)
    for c in range(2):
        rows[c, 3 * c] = 1.0
        rows[c, 3 * c + 1] = (degree + 2.0) / (2.0 * NMAX)
        rows[c, 3 * c + 2] = (degree + 2.0) * (degree + 1.0) / (6.0 * NMAX * NMAX)
    return rows


def local(heights, panels, ord_slot, cutoffs):
    keep = (degrees()[None, :] <= cutoffs[:, None]).astype(F32)
    back = main(heights, ord_slot, panels, keep, factor_rows())
    return inverse(back, ord_slot)


def solution(mesh):
    return jax.shard_map(
        local,
        mesh=mesh,
        in_specs=(P(("lat", "ord"), None), P("lat", "ord", None), P(), P("ord")),
        out_specs=P(("lat", "ord"), None),
        check_vma=False,
    )
```

time: 159 us -> 111 us (0.70)
  Pallas kernels: 151 us -> 108 us
  local copies, waits for them, and re-layouts: 6.71 us -> 1.01 us
    pallas_call x2 -> x1, Pallas kernels: 118 us -> 86.8 us  [main(): pl.pallas_call(main_kernel, out_shape=jax.ShapeDtypeStruct((16 * ROWS_OUT...]
    pallas_call x1, Pallas kernels: 33 us -> 21.1 us  [inverse(): pl.pallas_call(inverse_kernel, out_shape=jax.ShapeDtypeStruct((CYC, LON),...]
    unnamed x28 -> x12, local copies, waits for them, and re-layouts: 6.71 us -> 1.01 us
where the time goes in v3:
time: 111 us; the launch traced here: 110 us
  Pallas kernels  108 us (97%)
  other arithmetic  1.47 us (1%)
    pallas_call x1, Pallas kernels, main(): pl.pallas_call(main_kernel, out_shape=jax.ShapeDtypeStruct((16 * ROWS_OUT...  86.8 us
    pallas_call x1, Pallas kernels, inverse(): pl.pallas_call(inverse_kernel, out_shape=jax.ShapeDtypeStruct((CYC, LON),...  21.1 us

profile of v3, /device:TPU:1, one launch (start us, length us, event | category | flops | bytes accessed | tf_op | source)
XLA Modules:
  0.0 110.5 jit_solution(9674625449694155447)
XLA Ops:
  0.0 1.5 %compare_convert_fusion.keep_ref = f32[320,128]{1,0:T(8,128)} fusion(s32[128]{0:T(128)} %constant.37, s32[320]{0:T(512)} %param.19), kind=kLoop, calls=%fused_computation | loop fusion | flops 81920 | bytes 165632 | tf_op jit(solution)/shard_map/convert_element_type | solution.py:502
  1.5 0.0 copy-start.1
  1.5 0.0 copy-start.2
  1.5 0.0 copy-start.3
  1.5 0.0 copy-start.4
  1.5 0.0 copy-start.5
  1.5 86.8 %main.1.msg_ref = bf16[768,256]{1,0:T(8,128)(2,1)} custom-call(s32[5120]{0:T(1024)} %slot_ref.3, bf16[16,43200]{1,0:T(8,128)(2,1)} %x_hbm.1, bf16[192,192]{1,0:T(8,128)(2,1)} %constant.25.clone.fh_hbm, bf16[192,192]{1,0:T(8,128)(2,1)} %constant.26.clone.fl_hbm, f32[2,96,256]{2,1,0:T(8,128)} %constant.27.clone.twist_hbm.twist_ref, ...), custom_call_target="tpu_custom_call" | custom-call | flops 20000000000 | bytes 24000000 | tf_op jit(solution)/shard_map/main/pallas_call | solution.py:372
  88.3 0.0 copy-done.1
  88.3 0.0 copy-done.2
  88.3 0.0 copy-done.3
  88.3 0.0 copy-done.4
  88.4 0.0 copy-done.5
  88.4 0.0 copy-start
  88.4 1.0 copy-done
  89.4 21.1 %inverse.1 = f32[16,43200]{1,0:T(8,128)} custom-call(s32[5120]{0:T(1024)S(1)} %copy-done.5, bf16[768,256]{1,0:T(8,128)(2,1)S(1)} %copy-done, bf16[256,512]{1,0:T(8,128)(2,1)S(1)} %copy-done.1, f32[2,96,256]{2,1,0:T(8,128)S(1)} %copy-done.2, bf16[192,192]{1,0:T(8,128)(2,1)S(1)} %copy-done.4, bf16[192,192]{1,0:T(8,128)(2,1)S(1)} %copy-done.3), custom_call_target="tpu_custom_call" | custom-call | tf_op jit(solution)/shard_map/inverse/pallas_call | solution.py:471
Async XLA Ops:
  1.5 86.8 %copy-start.1 = (bf16[256,512]{1,0:T(8,128)(2,1)S(1)}, bf16[256,512]{1,0:T(8,128)(2,1)}, u32[]{:S(2)}) copy-start(bf16[256,512]{1,0:T(8,128)(2,1)} %constant.33.clone.back_ref) | copy-start | bytes 786436
  1.5 86.8 %copy-start.2 = (f32[2,96,256]{2,1,0:T(8,128)S(1)}, f32[2,96,256]{2,1,0:T(8,128)}, u32[]{:S(2)}) copy-start(f32[2,96,256]{2,1,0:T(8,128)} %constant.27.clone.twist_hbm.twist_ref) | copy-start | bytes 589828
  1.5 86.9 %copy-start.3 = (bf16[192,192]{1,0:T(8,128)(2,1)S(1)}, bf16[192,192]{1,0:T(8,128)(2,1)}, u32[]{:S(2)}) copy-start(bf16[192,192]{1,0:T(8,128)(2,1)} %constant.35.clone.ll_ref) | copy-start | bytes 221188
  1.5 86.9 %copy-start.4 = (bf16[192,192]{1,0:T(8,128)(2,1)S(1)}, bf16[192,192]{1,0:T(8,128)(2,1)}, u32[]{:S(2)}) copy-start(bf16[192,192]{1,0:T(8,128)(2,1)} %constant.34.clone.lh_ref) | copy-start | bytes 221188
  1.5 86.9 %copy-start.5 = (s32[5120]{0:T(1024)S(1)}, s32[5120]{0:T(1024)}, u32[]{:S(2)}) copy-start(s32[5120]{0:T(1024)} %slot_ref.3) | copy-start | bytes 61444
  88.4 1.0 copy-start

commit v4 on v3

--- a/solution.py
+++ b/solution.py
@@ -59,8 +59,9 @@
     second[1, :FAST, 0, 32:61] = -np.sin(bq1)
     second[0, :FAST, 1, 32:61] = -np.sin(bq1)
     second[1, :FAST, 1, 32:61] = -np.cos(bq1)
-    second[..., 64:] = second[..., :64]
-    second = second.reshape(512, 256) / math.sqrt(LON)
+    second = second / math.sqrt(LON)
+    high, low = split16(second[..., :64])
+    second = np.concatenate([high, low], -1).reshape(512, 256)
     back = np.zeros((2, 2, 32, 2, 256))
     back[0, 0, :29, 0, :FAST] = np.cos(bq).T
     back[0, 0, :29, 1, :FAST] = np.sin(bq).T
@@ -78,9 +79,9 @@
     rows = np.arange(128)
     lanes = np.arange(256)
     diag = (lanes[None, :] % 16 == rows[:, None] // 8).astype(jnp.bfloat16)
-    pick = (lanes[None, :] % 16 == np.arange(32)[:, None] % 16).astype(np.float32)
+    pick = (lanes[None, :] % 16 == np.arange(16)[:, None]).astype(np.float32)
     return dict(
-        first=split16(first), twist=twist, second=split16(second), back=back,
+        first=split16(first), twist=twist, second=second, back=back,
         last=split16(last), diag=diag, pick=pick,
     )
 
@@ -119,10 +120,10 @@
 SLAB = 80
 
 
-def main_kernel(slot_ref, x_hbm, fh_hbm, fl_hbm, twist_hbm, sh_hbm, sl_hbm, panel_ref, keep_ref, diag_ref,
+def main_kernel(slot_ref, cut_ref, x_hbm, fh_hbm, fl_hbm, twist_hbm, second_hbm, panel_ref, diag_ref,
                 factor_ref, pick_ref, out_ref,
-                x_ref, fh_ref, fl_ref, twist_ref, sh_ref, sl_ref, xs, qs, ts, gs, msg_ref,
-                pan, got, mine, parts, coeff, syn,
+                x_ref, fh_ref, fl_ref, twist_ref, second_ref, xs, qs, ts, gs, msg_ref,
+                pan, got, mine, parts, coeff, keeps, wide, syn,
                 xsem, tsem, psem, s1, r1, s2, r2, s3, r3, s4, r4):
     lat = lax.axis_index("lat")
     me = lax.axis_index("ord")
@@ -146,29 +147,33 @@
             device_id=(lat, ahead(d)), device_id_type=MESH,
         )
 
-    def slab_copy(d):
+    base = (0, 256, 512)
+    share = (32, 32, 16)
+
+    def slab_copy(T, d):
         peer = (lat + d) % 8
+        size = share[T]
         return pltpu.make_async_remote_copy(
-            src_ref=mine.at[pl.ds(pl.multiple_of(peer * SLAB, 16), SLAB)],
-            dst_ref=parts.at[pl.ds(pl.multiple_of(lat * SLAB, 16), SLAB)],
-            send_sem=s2.at[d], recv_sem=r2.at[d],
+            src_ref=mine.at[pl.ds(pl.multiple_of(base[T] + peer * size, 16), size)],
+            dst_ref=parts.at[pl.ds(pl.multiple_of(base[T] + lat * size, 16), size)],
+            send_sem=s2.at[T, d], recv_sem=r2.at[T, d],
             device_id=(peer, me), device_id_type=MESH,
         )
 
-    def coeff_copy(d):
+    def coeff_copy(T, d):
         peer = (lat + d) % 8
-        place = pl.ds(pl.multiple_of(lat * SLAB, 16), SLAB)
+        place = pl.ds(pl.multiple_of(base[T] + lat * share[T], 16), share[T])
         return pltpu.make_async_remote_copy(
             src_ref=coeff.at[place], dst_ref=coeff.at[place],
-            send_sem=s3.at[d], recv_sem=r3.at[d],
+            send_sem=s3.at[T, d], recv_sem=r3.at[T, d],
             device_id=(peer, me), device_id_type=MESH,
         )
 
-    def out_copy(d):
+    def out_copy(T, d):
         return pltpu.make_async_remote_copy(
-            src_ref=syn.at[pl.ds(pl.multiple_of(ahead(d) * ROWS_OUT, 16), ROWS_OUT)],
-            dst_ref=out_ref.at[pl.ds(pl.multiple_of(me * ROWS_OUT, 16), ROWS_OUT)],
-            send_sem=s4.at[d], recv_sem=r4.at[d],
+            src_ref=syn.at[pl.ds(pl.multiple_of(ahead(d) * ROWS_OUT + T * 16, 16), 16)],
+            dst_ref=out_ref.at[pl.ds(pl.multiple_of(me * ROWS_OUT + T * 16, 16), 16)],
+            send_sem=s4.at[T, d], recv_sem=r4.at[T, d],
             device_id=(lat, ahead(d)), device_id_type=MESH,
         )
 
@@ -180,17 +185,24 @@
 
     heights_copy = pltpu.make_async_copy(x_hbm, x_ref, xsem)
     heights_copy.start()
-    held = ((fh_hbm, fh_ref), (fl_hbm, fl_ref), (twist_hbm, twist_ref), (sh_hbm, sh_ref), (sl_hbm, sl_ref))
+    held = ((fh_hbm, fh_ref), (fl_hbm, fl_ref), (twist_hbm, twist_ref), (second_hbm, second_ref))
 
     def table_copy(i):
         return pltpu.make_async_copy(held[i][0], held[i][1], tsem.at[i])
 
-    for i in range(5):
+    for i in range(4):
         table_copy(i).start()
     loop(0, 16, lambda d: panel_copy(d).start())
     barrier = pltpu.get_barrier_semaphore()
     loop(1, 16, lambda d: pl.semaphore_signal(barrier, inc=1, device_id=(lat, ahead(d)), device_id_type=MESH))
     loop(1, 8, lambda d: pl.semaphore_signal(barrier, inc=1, device_id=((lat + d) % 8, me), device_id_type=MESH))
+    degree = ORDERS + (NMAX - ORDERS) // DEG * lax.broadcasted_iota(jnp.int32, (1, DEG), 1)
+    for T in range(3):
+        size = share[T]
+        for i in range(size):
+            slot = T * 128 + (lat * size + i) % (4 * size)
+            row = T * 32 + i
+            keeps[row : row + 1, :] = jnp.where(degree <= cut_ref[slot], 1.0, 0.0)
     heights_copy.wait()
     inside = lax.broadcasted_iota(jnp.int32, (CYC, 256), 1) < FAST
     for r in range(CYC):
@@ -230,15 +242,16 @@
             tc, tsin = twist_ref[0], twist_ref[1]
             z = jnp.concatenate([re * tc + im * tsin, im * tc - re * tsin], 1)
             zh, zl = halves(z)
-            o = dot(zh, sh_ref[...]) + dot(zh, sl_ref[...]) + dot(zl, sh_ref[...])
+            o = dot(zh, second_ref[...]) + dot(zl, second_ref[...])
             for c in range(2):
                 part = o[:, c * 128 : c * 128 + 128]
+                part = part + pltpu.roll(part, 64, 1)
                 qs[pl.ds(r * 8 + c * 3 + p, 48, stride=128), :] = jnp.where(first, part[:48], part[48:])
         for x in (6, 7):
             qs[pl.ds(r * 8 + x, 48, stride=128), :] = jnp.zeros((48, 128), F32)
         return carry
 
-    for i in range(5):
+    for i in range(4):
         table_copy(i).wait()
     lax.fori_loop(0, CYC, one_cycle, 0)
 
@@ -293,7 +306,7 @@
     loop(0, 16, lambda d: panel_copy(d).wait())
     loop(1, 16, lambda d: in_copy(d).wait_recv())
 
-    def analyse(i):
+    def analyse(T, i):
         accs = [None, None]
         for R in range(16):
             both = got[pl.ds(pl.multiple_of(R * ROWS_IN + i * 16, 16), 16), :].astype(F32)
@@ -309,62 +322,81 @@
         for e in range(2):
             rows = accs[e].reshape(16, 8, DEG)
             for c in range(2):
-                mine[pl.ds(pl.multiple_of(c * 320 + i * 32 + e * 16, 16), 16), :] = jnp.sum(
-                    rows * factor_ref[c][None], axis=1
-                )
-
-    loop(0, 10, analyse)
-    loop(1, 8, lambda d: slab_copy(d).start())
-    own = pl.ds(pl.multiple_of(lat * SLAB, 16), SLAB)
-    total = mine[own, :]
-    for d in range(1, 8):
-        slab_copy(d).wait_recv()
-        total = total + parts[pl.ds(pl.multiple_of((lat + 8 - d) % 8 * SLAB, 16), SLAB), :]
-    keep = keep_ref[pl.ds(pl.multiple_of(lat % 4 * SLAB, 16), SLAB), :]
-    coeff[own, :] = (total * keep).astype(BF16)
-    loop(1, 8, lambda d: coeff_copy(d).start())
-    loop(1, 8, lambda d: coeff_copy(d).wait_recv())
-
-    def synthesise(ref, peer, row):
-        def four(i):
-            outs = []
-            for e in range(8):
-                g = jnp.minimum(i * 8 + e, 19)
-                left = jnp.concatenate(
-                    [coeff[pl.ds(pl.multiple_of(c * 320 + g * 16, 16), 16), :] for c in range(2)], 0
-                )
-                right = pan[
-                    pl.ds(pl.multiple_of(peer * 16, 16), 16), pl.ds(pl.multiple_of(g * 16, 16), 16), :
-                ].reshape(256, DEG)
-                d = lax.dot_general(left, right, (((1,), (1,)), ((), ())), preferred_element_type=F32)
-                d = d * pick_ref[...]
-                for c in range(2):
-                    outs.append(jnp.sum(d[c * 16 : c * 16 + 16], axis=0, keepdims=True))
-            ref[pl.ds(pl.multiple_of(row * ROWS_OUT + i * 16, 16), 16), :] = jnp.concatenate(outs, 0).astype(BF16)
-        loop(0, 3, four)
-
-    def leaving(i):
-        d = 16 - i
-        synthesise(syn, ahead(d), ahead(d))
-        out_copy(d).start()
-
-    loop(1, 16, leaving)
-    synthesise(out_ref, me, me)
-
-    def finish(d):
-        in_copy(d).wait_send()
-        out_copy(d).wait()
-
-    loop(1, 16, finish)
-
-    def finish_lat(d):
-        slab_copy(d).wait_send()
-        coeff_copy(d).wait_send()
-
-    loop(1, 8, finish_lat)
-
-
-def main(heights, slots, panels, keep, factors):
+                row = base[T] + c * 4 * share[T] + (i - 4 * T) * 32 + e * 16
+                mine[pl.ds(pl.multiple_of(row, 16), 16), :] = jnp.sum(rows * factor_ref[c][None], axis=1)
+
+    def analyse_part(T):
+        loop(4 * T, min(4 * T + 4, 10), lambda i: analyse(T, i))
+        loop(1, 8, lambda d: slab_copy(T, d).start())
+
+    def total_part(T):
+        size = share[T]
+        own = pl.ds(pl.multiple_of(base[T] + lat * size, 16), size)
+        total = mine[own, :]
+        for d in range(1, 8):
+            slab_copy(T, d).wait_recv()
+            total = total + parts[pl.ds(pl.multiple_of(base[T] + (lat + 8 - d) % 8 * size, 16), size), :]
+        coeff[own, :] = (total * keeps[T * 32 : T * 32 + size, :]).astype(BF16)
+        loop(1, 8, lambda d: coeff_copy(T, d).start())
+
+    chunk = lax.broadcasted_iota(jnp.int32, (DEG, 128), 1) // 16
+
+    def synthesis_part(T):
+        groups = share[T] // 4
+        loop(1, 8, lambda d: coeff_copy(T, d).wait_recv())
+        for c in range(2):
+            rows = coeff[base[T] + c * groups * 16 : base[T] + (c + 1) * groups * 16, :].astype(F32)
+            if groups < 8:
+                rows = jnp.concatenate([rows, jnp.zeros((128 - groups * 16, DEG), F32)], 0)
+            turned = rows.T
+            for g in range(groups):
+                wide[g * DEG : g * DEG + DEG, c * 128 : c * 128 + 128] = jnp.where(
+                    chunk == g, turned, 0.0
+                ).astype(BF16)
+
+        def one_peer(ref, peer, row):
+            left = jnp.concatenate(
+                [
+                    pan[
+                        pl.ds(pl.multiple_of(peer * 16, 16), 16), T * 128 + g * 16 : T * 128 + g * 16 + 16, :
+                    ].reshape(256, DEG)
+                    for g in range(groups)
+                ],
+                1,
+            )
+            o = dot(left, wide[: groups * DEG, :]).reshape(16, 16, 256)
+            o = jnp.sum(o * pick_ref[...][None], axis=1)
+            ref[pl.ds(pl.multiple_of(row * ROWS_OUT + T * 16, 16), 16), :] = o.astype(BF16)
+
+        def leaving(i):
+            d = 16 - i
+            one_peer(syn, ahead(d), ahead(d))
+            out_copy(T, d).start()
+
+        loop(1, 16, leaving)
+        one_peer(out_ref, me, me)
+
+    analyse_part(0)
+    analyse_part(1)
+    total_part(0)
+    analyse_part(2)
+    total_part(1)
+    synthesis_part(0)
+    total_part(2)
+    synthesis_part(1)
+    synthesis_part(2)
+    loop(1, 16, lambda d: in_copy(d).wait_send())
+    for T in range(3):
+        loop(1, 16, lambda d: out_copy(T, d).wait())
+
+        def finish_lat(d):
+            slab_copy(T, d).wait_send()
+            coeff_copy(T, d).wait_send()
+
+        loop(1, 8, finish_lat)
+
+
+def main(heights, slots, cutoffs, panels, factors):
     t = tables()
     dma = pltpu.SemaphoreType.DMA
     vec = pltpu.VMEM
@@ -372,14 +404,13 @@
     return pl.pallas_call(
         main_kernel,
         out_shape=jax.ShapeDtypeStruct((16 * ROWS_OUT, 256), BF16),
-        in_specs=[pl.BlockSpec(memory_space=pltpu.SMEM)] + [hbm] * 7 + [vmem()] * 4,
+        in_specs=[pl.BlockSpec(memory_space=pltpu.SMEM)] * 2 + [hbm] * 6 + [vmem()] * 3,
         out_specs=vmem(),
         scratch_shapes=[
             vec((CYC, LON), BF16),
             vec((192, 192), BF16),
             vec((192, 192), BF16),
             vec((2, HALF, 256), F32),
-            vec((512, 256), BF16),
             vec((512, 256), BF16),
             vec((2, CYC * 192, 128), F32),
             vec((48 * 128, 128), F32),
@@ -391,39 +422,29 @@
             vec((640, DEG), F32),
             vec((640, DEG), F32),
             vec((640, DEG), BF16),
+            vec((80, DEG), F32),
+            vec((8 * DEG, 256), BF16),
             vec((16 * ROWS_OUT, 256), BF16),
-            dma, dma((5,)), dma((16,)), dma((16,)), dma((16,)), dma((8,)), dma((8,)), dma((8,)), dma((8,)),
-            dma((16,)), dma((16,)),
+            dma, dma((4,)), dma((16,)), dma((16,)), dma((16,)), dma((3, 8)), dma((3, 8)), dma((3, 8)), dma((3, 8)),
+            dma((3, 16)), dma((3, 16)),
         ],
         compiler_params=pltpu.CompilerParams(
             vmem_limit_bytes=56 * MIB, collective_id=0, has_side_effects=True
         ),
         cost_estimate=pl.CostEstimate(flops=2 * 10**10, bytes_accessed=24 * 10**6, transcendentals=0),
         name="main",
-    )(slots, heights, *t["first"], t["twist"], *t["second"], panels, keep, t["diag"], factors, t["pick"])
+    )(slots, cutoffs, heights, *t["first"], t["twist"], t["second"], panels, t["diag"], factors, t["pick"])
 
 
 def inverse_kernel(slot_ref, msg_ref, back_ref, twist_ref, lh_ref, ll_ref, out_ref, ts, ls, ys):
     ts[0:8, :] = jnp.zeros((8, 128), F32)
     ts[ORDERS:TROWS, :] = jnp.zeros((TROWS - ORDERS, 128), F32)
-
-    sub = lax.broadcasted_iota(jnp.int32, (8, 128), 0)
 
     def one_peer(o, carry):
         for part in range(3):
             rows = msg_ref[pl.ds(pl.multiple_of(o * 48 + part * 16, 16), 16), :].astype(F32)
             count = 128 if part < 2 else 64
-            groups = []
-            for g in range(8):
-                half = rows[g // 4 * 8 : g // 4 * 8 + 8]
-                v0, v1 = half[:, :128], half[:, 128:]
-                at = g % 4
-                v0 = pltpu.roll(v0, 8 - 2 * at, 0) if at else v0
-                v1 = pltpu.roll(v1, (10 - 2 * at) % 8, 0) if at != 1 else v1
-                groups.append(jnp.where(sub < 2, v0, v1))
-            blocks = swap_chunks(groups)
-            packed = [jnp.where(sub < 4, blocks[2 * i], pltpu.roll(blocks[2 * i + 1], 4, 0)) for i in range(4)]
-            t = jnp.concatenate(packed, 0).T
+            t = jnp.concatenate([rows[:, :128], rows[:, 128:]], 0).T
             base = o * 320 + part * 128
             for i in range(count):
                 ts[pl.ds(slot_ref[base + i] + 1, 1), 0:32] = t[i : i + 1]
@@ -441,13 +462,12 @@
         ls[pl.ds(k, 32, stride=48), :] = jnp.concatenate(stack, 0)[:, :32].T
         return carry
 
-    lax.fori_loop(0, 48, one_k, 0)
+    lax.fori_loop(0, 48, one_k, 0, unroll=4)
     first = lax.broadcasted_iota(jnp.int32, (48, 128), 1) < 64
 
     def one_cycle(r, carry):
-        at = (r % 8 * 4 + r // 8 * 2) * 48
-        l0 = ls[pl.ds(pl.multiple_of(at, 48), 48), :]
-        l1 = ls[pl.ds(pl.multiple_of(at + 48, 48), 48), :]
+        l0 = ls[pl.ds(pl.multiple_of(r * 48, 48), 48), :]
+        l1 = ls[pl.ds(pl.multiple_of((r + CYC) * 48, 48), 48), :]
         left = jnp.concatenate(
             [jnp.where(first, l0, pltpu.roll(l1, 64, 1)), jnp.where(first, pltpu.roll(l0, 64, 1), l1)], 0
         ).astype(BF16)
@@ -499,8 +519,7 @@
 
 
 def local(heights, panels, ord_slot, cutoffs):
-    keep = (degrees()[None, :] <= cutoffs[:, None]).astype(F32)
-    back = main(heights, ord_slot, panels, keep, factor_rows())
+    back = main(heights, ord_slot, cutoffs, panels, factor_rows())
     return inverse(back, ord_slot)
 
 

time: 111 us -> 100 us (0.901)
  Pallas kernels: 108 us -> 99.1 us
  other arithmetic: 1.47 us -> 0 us
    pallas_call x1, Pallas kernels: 21.1 us -> 15.7 us  [inverse(): pl.pallas_call(inverse_kernel, out_shape=jax.ShapeDtypeStruct((CYC, LON),...]
    pallas_call x1, Pallas kernels: 86.8 us -> 83.4 us  [main(): pl.pallas_call(main_kernel, out_shape=jax.ShapeDtypeStruct((16 * ROWS_OUT...]
    convert_element_type x1 -> x0, other arithmetic: 1.47 us -> none  [local(): keep = (degrees()[None, :] <= cutoffs[:, None]).astype(F32)]
where the time goes in v4:
time: 100 us
  Pallas kernels  99.1 us (99%)
  local copies, waits for them, and re-layouts  1.01 us (1%)
    pallas_call x1, Pallas kernels, main(): pl.pallas_call(main_kernel, out_shape=jax.ShapeDtypeStruct((16 * ROWS_OUT...  83.4 us
    pallas_call x1, Pallas kernels, inverse(): pl.pallas_call(inverse_kernel, out_shape=jax.ShapeDtypeStruct((CYC, LON),...  15.7 us

profile of v4, /device:TPU:1, one launch (start us, length us, event | category | flops | bytes accessed | tf_op | source)
XLA Modules:
  0.0 100.1 jit_solution(10260340880180312932)
XLA Ops:
  0.0 0.0 copy-start.1
  0.0 0.0 copy-start.2
  0.0 0.0 copy-start.3
  0.0 0.0 copy-start.4
  0.0 0.0 copy-start.5
  0.0 83.4 %main.1.msg_ref = bf16[768,256]{1,0:T(8,128)(2,1)} custom-call(s32[5120]{0:T(1024)} %slot_ref.3, s32[320]{0:T(512)} %cut_ref.1, bf16[16,43200]{1,0:T(8,128)(2,1)} %x_hbm.1, bf16[192,192]{1,0:T(8,128)(2,1)} %constant.20.clone.fh_hbm, bf16[192,192]{1,0:T(8,128)(2,1)} %constant.21.clone.fl_hbm, f32[2,96,256]{2,1,0:T(8,128)} %constant.22.clone.twist_hbm.twist_ref, ...), custom_call_target="tpu_custom_call" | custom-call | flops 20000000000 | bytes 24000000 | tf_op jit(solution)/shard_map/main/pallas_call | solution.py:404
  83.4 0.0 copy-done.1
  83.4 0.0 copy-done.2
  83.4 0.0 copy-done.3
  83.4 0.0 copy-done.4
  83.5 0.0 copy-done.5
  83.5 0.0 copy-start
  83.5 1.0 copy-done
  84.5 15.7 %inverse.1 = f32[16,43200]{1,0:T(8,128)} custom-call(s32[5120]{0:T(1024)S(1)} %copy-done.5, bf16[768,256]{1,0:T(8,128)(2,1)S(1)} %copy-done, bf16[256,512]{1,0:T(8,128)(2,1)S(1)} %copy-done.1, f32[2,96,256]{2,1,0:T(8,128)S(1)} %copy-done.2, bf16[192,192]{1,0:T(8,128)(2,1)S(1)} %copy-done.4, bf16[192,192]{1,0:T(8,128)(2,1)S(1)} %copy-done.3), custom_call_target="tpu_custom_call" | custom-call | tf_op jit(solution)/shard_map/inverse/pallas_call | solution.py:491
Async XLA Ops:
  0.0 83.4 %copy-start.1 = (bf16[256,512]{1,0:T(8,128)(2,1)S(1)}, bf16[256,512]{1,0:T(8,128)(2,1)}, u32[]{:S(2)}) copy-start(bf16[256,512]{1,0:T(8,128)(2,1)} %constant.27.clone.back_ref) | copy-start | bytes 786436
  0.0 83.4 %copy-start.2 = (f32[2,96,256]{2,1,0:T(8,128)S(1)}, f32[2,96,256]{2,1,0:T(8,128)}, u32[]{:S(2)}) copy-start(f32[2,96,256]{2,1,0:T(8,128)} %constant.22.clone.twist_hbm.twist_ref) | copy-start | bytes 589828
  0.0 83.4 %copy-start.3 = (bf16[192,192]{1,0:T(8,128)(2,1)S(1)}, bf16[192,192]{1,0:T(8,128)(2,1)}, u32[]{:S(2)}) copy-start(bf16[192,192]{1,0:T(8,128)(2,1)} %constant.29.clone.ll_ref) | copy-start | bytes 221188
  0.0 83.4 %copy-start.4 = (bf16[192,192]{1,0:T(8,128)(2,1)S(1)}, bf16[192,192]{1,0:T(8,128)(2,1)}, u32[]{:S(2)}) copy-start(bf16[192,192]{1,0:T(8,128)(2,1)} %constant.28.clone.lh_ref) | copy-start | bytes 221188
  0.0 83.4 %copy-start.5 = (s32[5120]{0:T(1024)S(1)}, s32[5120]{0:T(1024)}, u32[]{:S(2)}) copy-start(s32[5120]{0:T(1024)} %slot_ref.3) | copy-start | bytes 61444
  83.5 1.0 copy-start

commit v5 on v4

--- a/solution.py
+++ b/solution.py
@@ -115,7 +115,7 @@
 
 
 MESH = pl.DeviceIdType.MESH
-ROWS_IN = 160
+ROWS_IN = 80
 ROWS_OUT = 48
 SLAB = 80
 
@@ -123,7 +123,7 @@
 def main_kernel(slot_ref, cut_ref, x_hbm, fh_hbm, fl_hbm, twist_hbm, second_hbm, panel_ref, diag_ref,
                 factor_ref, pick_ref, out_ref,
                 x_ref, fh_ref, fl_ref, twist_ref, second_ref, xs, qs, ts, gs, msg_ref,
-                pan, got, mine, parts, coeff, keeps, wide, syn,
+                pan, got, acc, mine, parts, coeff, keeps, wide, syn,
                 xsem, tsem, psem, s1, r1, s2, r2, s3, r3, s4, r4):
     lat = lax.axis_index("lat")
     me = lax.axis_index("ord")
@@ -229,6 +229,8 @@
         rows = pl.ds(pl.multiple_of(r * 192, 192), 192)
         level = jnp.concatenate([xs[0, rows, :], xs[1, rows, :]], 1)
         value = level
+        stack = []
+        tc, tsin = twist_ref[0], twist_ref[1]
         for p in range(3):
             if p:
                 value = value * level
@@ -239,21 +241,19 @@
                 high, low = halves(value)
                 y = dot(fh_ref[...], high) + dot(fl_ref[...], high) + dot(fh_ref[...], low)
             re, im = y[:HALF], y[HALF:]
-            tc, tsin = twist_ref[0], twist_ref[1]
-            z = jnp.concatenate([re * tc + im * tsin, im * tc - re * tsin], 1)
-            zh, zl = halves(z)
-            o = dot(zh, second_ref[...]) + dot(zl, second_ref[...])
+            stack += list(halves(jnp.concatenate([re * tc + im * tsin, im * tc - re * tsin], 1)))
+        o = dot(jnp.concatenate(stack, 0), second_ref[...])
+        for p in range(3):
+            both = o[p * 192 : p * 192 + HALF] + o[p * 192 + HALF : p * 192 + 192]
             for c in range(2):
-                part = o[:, c * 128 : c * 128 + 128]
+                part = both[:, c * 128 : c * 128 + 128]
                 part = part + pltpu.roll(part, 64, 1)
                 qs[pl.ds(r * 8 + c * 3 + p, 48, stride=128), :] = jnp.where(first, part[:48], part[48:])
-        for x in (6, 7):
-            qs[pl.ds(r * 8 + x, 48, stride=128), :] = jnp.zeros((48, 128), F32)
         return carry
 
     for i in range(4):
         table_copy(i).wait()
-    lax.fori_loop(0, CYC, one_cycle, 0)
+    lax.fori_loop(0, CYC, one_cycle, 0, unroll=2)
 
     def one_k(k, carry):
         t = qs[pl.ds(pl.multiple_of(k * 128, 128), 128), :].T
@@ -276,8 +276,10 @@
 
     pl.semaphore_wait(barrier, 22)
 
+    sub = lax.broadcasted_iota(jnp.int32, (8, 128), 0)
+
     def one_chip(i, carry):
-        far = 7 - i
+        far = 7 - i // 2 - i % 2 * 4
         chip = (hy + far // 4) % 2 * 4 + (hz + far % 4) % 4
         for j in range(5):
             tile = chip * 5 + j
@@ -286,12 +288,16 @@
                 for e in range(32):
                     gs[j, i + e : i + e + 1, :] = rows[e]
             t = gs[j].T
-            sides = []
-            for h in range(2):
-                sides.append(
-                    jnp.concatenate(swap_chunks([t[(h * 8 + r) * 8 : (h * 8 + r + 1) * 8] for r in range(8)]), 0)
-                )
-            msg_ref[pl.ds(pl.multiple_of(tile * 64, 64), 64), :] = jnp.concatenate(sides, 1).astype(BF16)
+            sides = [swap_chunks([t[(h * 8 + r) * 8 : (h * 8 + r + 1) * 8] for r in range(8)]) for h in range(2)]
+            rows = []
+            for u in (0, 4):
+                for side in sides:
+                    rows.append(
+                        jnp.concatenate(
+                            [jnp.where(sub < 6, side[u + v], pltpu.roll(side[u + 3], 6 - 2 * v, 0)) for v in range(3)], 1
+                        )
+                    )
+            msg_ref[pl.ds(pl.multiple_of(tile * 32, 32), 32), :] = jnp.concatenate(rows, 0).astype(BF16)
 
         @pl.when(far > 0)
         def _():
@@ -304,29 +310,59 @@
     own_in = pl.ds(pl.multiple_of(me * ROWS_IN, 16), ROWS_IN)
     got[own_in, :] = msg_ref[own_in, :]
     loop(0, 16, lambda d: panel_copy(d).wait())
-    loop(1, 16, lambda d: in_copy(d).wait_recv())
-
-    def analyse(T, i):
-        accs = [None, None]
-        for R in range(16):
-            both = got[pl.ds(pl.multiple_of(R * ROWS_IN + i * 16, 16), 16), :].astype(F32)
-            for e in range(2):
-                one = both[e * 8 : e * 8 + 8]
-                two = jnp.concatenate([one, one], 0).astype(BF16)
-                left = jnp.concatenate([two] * 8, 0) * diag_ref[...]
-                right = pan[
-                    R * 16 : R * 16 + 16, pl.ds(pl.multiple_of(i * 32 + e * 16, 16), 16), :
-                ].reshape(256, DEG)
-                d = dot(left, right)
-                accs[e] = d if R == 0 else accs[e] + d
-        for e in range(2):
-            rows = accs[e].reshape(16, 8, DEG)
+    def contract(q, far_set):
+        sums = []
+        for pair in range(2):
+            accs = [None, None]
+            for d in far_set:
+                peer = behind(d)
+                rows = got[pl.ds(pl.multiple_of(peer * ROWS_IN + q * 16, 16), 16), :].astype(F32)
+                for e in range(2):
+                    v = pair * 2 + e
+                    sides = []
+                    for h in (0, 8):
+                        if v < 3:
+                            sides.append(rows[h : h + 8, v * 128 : v * 128 + 128])
+                        else:
+                            x, y, z = (
+                                pltpu.roll(rows[h : h + 8, w * 128 : w * 128 + 128], 2 + 2 * w, 0) for w in range(3)
+                            )
+                            sides.append(jnp.where(sub < 2, x, jnp.where(sub < 4, y, z)))
+                    one = jnp.concatenate(sides, 1)
+                    two = jnp.concatenate([one, one], 0).astype(BF16)
+                    left = jnp.concatenate([two] * 8, 0) * diag_ref[...]
+                    right = pan[
+                        pl.ds(pl.multiple_of(peer * 16, 16), 16), pl.ds(pl.multiple_of(q * 64 + v * 16, 16), 16), :
+                    ].reshape(256, DEG)
+                    t = dot(left, right)
+                    accs[e] = t if accs[e] is None else accs[e] + t
+            sums += accs
+        return sums
+
+    early = (14, 15, 6, 7, 12, 13, 4, 5)
+    late = (10, 11, 2, 3, 8, 9, 0, 1)
+
+    def first_half(q):
+        for v, t in enumerate(contract(q, early)):
+            acc[pl.ds(pl.multiple_of(q * 512 + v * 128, 128), 128), :] = t
+
+    def second_half(T, q):
+        for v, t in enumerate(contract(q, late)):
+            t = t + acc[pl.ds(pl.multiple_of(q * 512 + v * 128, 128), 128), :]
+            rows = t.reshape(16, 8, DEG)
             for c in range(2):
-                row = base[T] + c * 4 * share[T] + (i - 4 * T) * 32 + e * 16
+                row = base[T] + c * 4 * share[T] + (q - 2 * T) * 64 + v * 16
                 mine[pl.ds(pl.multiple_of(row, 16), 16), :] = jnp.sum(rows * factor_ref[c][None], axis=1)
 
+    for d in early:
+        in_copy(d).wait_recv()
+    loop(0, 5, first_half)
+    for d in late:
+        if d:
+            in_copy(d).wait_recv()
+
     def analyse_part(T):
-        loop(4 * T, min(4 * T + 4, 10), lambda i: analyse(T, i))
+        loop(2 * T, min(2 * T + 2, 5), lambda q: second_half(T, q))
         loop(1, 8, lambda d: slab_copy(T, d).start())
 
     def total_part(T):
@@ -416,9 +452,10 @@
             vec((48 * 128, 128), F32),
             vec((TROWS, 128), F32),
             vec((5, 128, 128), F32),
-            vec((16 * ROWS_IN, 256), BF16),
+            vec((16 * ROWS_IN, 384), BF16),
             vec((256, 320, DEG), BF16),
-            vec((16 * ROWS_IN, 256), BF16),
+            vec((16 * ROWS_IN, 384), BF16),
+            vec((20 * 128, DEG), F32),
             vec((640, DEG), F32),
             vec((640, DEG), F32),
             vec((640, DEG), BF16),

time: 100 us -> 90.2 us (0.902)
  Pallas kernels: 99.1 us -> 88.9 us
    pallas_call x1, Pallas kernels: 83.4 us -> 73.3 us  [main(): pl.pallas_call(main_kernel, out_shape=jax.ShapeDtypeStruct((16 * ROWS_OUT...]
where the time goes in v5:
time: 90.2 us; the launch traced here: 90 us
  Pallas kernels  88.9 us (99%)
  local copies, waits for them, and re-layouts  1.01 us (1%)
    pallas_call x1, Pallas kernels, main(): pl.pallas_call(main_kernel, out_shape=jax.ShapeDtypeStruct((16 * ROWS_OUT...  73.3 us
    pallas_call x1, Pallas kernels, inverse(): pl.pallas_call(inverse_kernel, out_shape=jax.ShapeDtypeStruct((CYC, LON),...  15.7 us

profile of v5, /device:TPU:1, one launch (start us, length us, event | category | flops | bytes accessed | tf_op | source)
XLA Modules:
  0.0 90.0 jit_solution(6834354597227998675)
XLA Ops:
  0.0 0.0 copy-start.1
  0.0 0.0 copy-start.2
  0.0 0.0 copy-start.3
  0.0 0.0 copy-start.4
  0.0 0.0 copy-start.5
  0.0 73.3 %main.1.msg_ref = bf16[768,256]{1,0:T(8,128)(2,1)} custom-call(s32[5120]{0:T(1024)} %slot_ref.3, s32[320]{0:T(512)} %cut_ref.1, bf16[16,43200]{1,0:T(8,128)(2,1)} %x_hbm.1, bf16[192,192]{1,0:T(8,128)(2,1)} %constant.20.clone.fh_hbm, bf16[192,192]{1,0:T(8,128)(2,1)} %constant.21.clone.fl_hbm, f32[2,96,256]{2,1,0:T(8,128)} %constant.22.clone.twist_hbm.twist_ref, ...), custom_call_target="tpu_custom_call" | custom-call | flops 20000000000 | bytes 24000000 | tf_op jit(solution)/shard_map/main/pallas_call | solution.py:440
  73.3 0.0 copy-done.1
  73.3 0.0 copy-done.2
  73.3 0.0 copy-done.3
  73.3 0.0 copy-done.4
  73.4 0.0 copy-done.5
  73.4 0.0 copy-start
  73.4 1.0 %copy-done = bf16[768,256]{1,0:T(8,128)(2,1)S(1)} copy-done((bf16[768,256]{1,0:T(8,128)(2,1)S(1)}, bf16[768,256]{1,0:T(8,128)(2,1)}, u32[]{:S(2)}) %copy-start) | copy-done | bytes 393240
  74.4 15.7 %inverse.1 = f32[16,43200]{1,0:T(8,128)} custom-call(s32[5120]{0:T(1024)S(1)} %copy-done.5, bf16[768,256]{1,0:T(8,128)(2,1)S(1)} %copy-done, bf16[256,512]{1,0:T(8,128)(2,1)S(1)} %copy-done.1, f32[2,96,256]{2,1,0:T(8,128)S(1)} %copy-done.2, bf16[192,192]{1,0:T(8,128)(2,1)S(1)} %copy-done.4, bf16[192,192]{1,0:T(8,128)(2,1)S(1)} %copy-done.3), custom_call_target="tpu_custom_call" | custom-call | tf_op jit(solution)/shard_map/inverse/pallas_call | solution.py:528
Async XLA Ops:
  0.0 73.3 %copy-start.1 = (bf16[256,512]{1,0:T(8,128)(2,1)S(1)}, bf16[256,512]{1,0:T(8,128)(2,1)}, u32[]{:S(2)}) copy-start(bf16[256,512]{1,0:T(8,128)(2,1)} %constant.27.clone.back_ref) | copy-start | bytes 786436
  0.0 73.3 %copy-start.2 = (f32[2,96,256]{2,1,0:T(8,128)S(1)}, f32[2,96,256]{2,1,0:T(8,128)}, u32[]{:S(2)}) copy-start(f32[2,96,256]{2,1,0:T(8,128)} %constant.22.clone.twist_hbm.twist_ref) | copy-start | bytes 589828
  0.0 73.3 %copy-start.3 = (bf16[192,192]{1,0:T(8,128)(2,1)S(1)}, bf16[192,192]{1,0:T(8,128)(2,1)}, u32[]{:S(2)}) copy-start(bf16[192,192]{1,0:T(8,128)(2,1)} %constant.29.clone.ll_ref) | copy-start | bytes 221188
  0.0 73.3 %copy-start.4 = (bf16[192,192]{1,0:T(8,128)(2,1)S(1)}, bf16[192,192]{1,0:T(8,128)(2,1)}, u32[]{:S(2)}) copy-start(bf16[192,192]{1,0:T(8,128)(2,1)} %constant.28.clone.lh_ref) | copy-start | bytes 221188
  0.0 73.3 %copy-start.5 = (s32[5120]{0:T(1024)S(1)}, s32[5120]{0:T(1024)}, u32[]{:S(2)}) copy-start(s32[5120]{0:T(1024)} %slot_ref.3) | copy-start | bytes 61444
  73.4 1.0 %copy-start = (bf16[768,256]{1,0:T(8,128)(2,1)S(1)}, bf16[768,256]{1,0:T(8,128)(2,1)}, u32[]{:S(2)}) copy-start(bf16[768,256]{1,0:T(8,128)(2,1)} %main.1.msg_ref) | copy-start | bytes 1179652

commit v6 on v5

--- a/solution.py
+++ b/solution.py
@@ -192,7 +192,6 @@
 
     for i in range(4):
         table_copy(i).start()
-    loop(0, 16, lambda d: panel_copy(d).start())
     barrier = pltpu.get_barrier_semaphore()
     loop(1, 16, lambda d: pl.semaphore_signal(barrier, inc=1, device_id=(lat, ahead(d)), device_id_type=MESH))
     loop(1, 8, lambda d: pl.semaphore_signal(barrier, inc=1, device_id=((lat + d) % 8, me), device_id_type=MESH))
@@ -253,10 +252,11 @@
 
     for i in range(4):
         table_copy(i).wait()
+    loop(0, 16, lambda d: panel_copy(d).start())
     lax.fori_loop(0, CYC, one_cycle, 0, unroll=2)
 
     def one_k(k, carry):
-        t = qs[pl.ds(pl.multiple_of(k * 128, 128), 128), :].T
+        t = qs[pl.ds(k * 128 if isinstance(k, int) else pl.multiple_of(k * 128, 128), 128), :].T
         ts[pl.ds(k, 32, stride=SLOW), :] = t[0:32]
         ts[pl.ds(SLOW - k, 32, stride=SLOW), :] = t[32:64]
         return t
@@ -267,12 +267,11 @@
         ts[pl.ds(SLOW - 48 - k, 32, stride=SLOW), :] = t[96:128]
         return carry
 
-    def only_k(k, carry):
-        one_k(k, carry)
-        return carry
-
-    lax.fori_loop(0, 43, two_k, 0)
-    lax.fori_loop(43, 48, only_k, 0)
+    lax.fori_loop(0, 40, two_k, 0, unroll=4)
+    for k in range(40, 43):
+        two_k(k, 0)
+    for k in range(43, 48):
+        one_k(k, 0)
 
     pl.semaphore_wait(barrier, 22)
 
@@ -390,27 +389,38 @@
                     chunk == g, turned, 0.0
                 ).astype(BF16)
 
-        def one_peer(ref, peer, row):
+        def two_peers(d, refs):
             left = jnp.concatenate(
                 [
-                    pan[
-                        pl.ds(pl.multiple_of(peer * 16, 16), 16), T * 128 + g * 16 : T * 128 + g * 16 + 16, :
-                    ].reshape(256, DEG)
-                    for g in range(groups)
+                    jnp.concatenate(
+                        [
+                            pan[
+                                pl.ds(pl.multiple_of(ahead(d + e) * 16, 16), 16),
+                                T * 128 + g * 16 : T * 128 + g * 16 + 16, :
+                            ].reshape(256, DEG)
+                            for g in range(groups)
+                        ],
+                        1,
+                    )
+                    for e in range(2)
                 ],
-                1,
+                0,
             )
-            o = dot(left, wide[: groups * DEG, :]).reshape(16, 16, 256)
+            o = dot(left, wide[: groups * DEG, :]).reshape(32, 16, 256)
             o = jnp.sum(o * pick_ref[...][None], axis=1)
-            ref[pl.ds(pl.multiple_of(row * ROWS_OUT + T * 16, 16), 16), :] = o.astype(BF16)
+            for e in range(2):
+                place = pl.ds(pl.multiple_of(ahead(d + e) * ROWS_OUT + T * 16, 16), 16)
+                refs[e][place, :] = o[e * 16 : e * 16 + 16].astype(BF16)
 
         def leaving(i):
-            d = 16 - i
-            one_peer(syn, ahead(d), ahead(d))
+            d = 16 - 2 * i
+            two_peers(d, (syn, syn))
             out_copy(T, d).start()
-
-        loop(1, 16, leaving)
-        one_peer(out_ref, me, me)
+            out_copy(T, d + 1).start()
+
+        loop(1, 8, leaving)
+        two_peers(0, (out_ref, syn))
+        out_copy(T, 1).start()
 
     analyse_part(0)
     analyse_part(1)
@@ -473,7 +483,12 @@
     )(slots, cutoffs, heights, *t["first"], t["twist"], t["second"], panels, t["diag"], factors, t["pick"])
 
 
-def inverse_kernel(slot_ref, msg_ref, back_ref, twist_ref, lh_ref, ll_ref, out_ref, ts, ls, ys):
+def inverse_kernel(slot_ref, msg_ref, back_hbm, twist_hbm, lh_hbm, ll_hbm, out_hbm,
+                   back_ref, twist_ref, lh_ref, ll_ref, out_ref, ts, ls, ys, tsem, osem):
+    held = ((back_hbm, back_ref), (twist_hbm, twist_ref), (lh_hbm, lh_ref), (ll_hbm, ll_ref))
+    copies = [pltpu.make_async_copy(held[i][0], held[i][1], tsem.at[i]) for i in range(4)]
+    for copy in copies:
+        copy.start()
     ts[0:8, :] = jnp.zeros((8, 128), F32)
     ts[ORDERS:TROWS, :] = jnp.zeros((TROWS - ORDERS, 128), F32)
 
@@ -502,25 +517,39 @@
     lax.fori_loop(0, 48, one_k, 0, unroll=4)
     first = lax.broadcasted_iota(jnp.int32, (48, 128), 1) < 64
 
-    def one_cycle(r, carry):
-        l0 = ls[pl.ds(pl.multiple_of(r * 48, 48), 48), :]
-        l1 = ls[pl.ds(pl.multiple_of((r + CYC) * 48, 48), 48), :]
-        left = jnp.concatenate(
-            [jnp.where(first, l0, pltpu.roll(l1, 64, 1)), jnp.where(first, pltpu.roll(l0, 64, 1), l1)], 0
-        ).astype(BF16)
+    def four_cycles(step, carry):
+        lefts = []
+        for i in range(4):
+            r = step * 4 + i
+            l0 = ls[pl.ds(pl.multiple_of(r * 48, 48), 48), :]
+            l1 = ls[pl.ds(pl.multiple_of((r + CYC) * 48, 48), 48), :]
+            lefts += [jnp.where(first, l0, pltpu.roll(l1, 64, 1)), jnp.where(first, pltpu.roll(l0, 64, 1), l1)]
+        left = jnp.concatenate(lefts, 0).astype(BF16)
         w = dot(jnp.concatenate([left, left], 1), back_ref[...])
-        re, im = w[:, :256], w[:, 256:]
         c, s = twist_ref[0], twist_ref[1]
-        v = jnp.concatenate([re * c - im * s, im * c + re * s], 0).astype(BF16)
-        field = dot(lh_ref[...], v) + dot(ll_ref[...], v)
-        for lane in range(2):
-            ys[lane, pl.ds(pl.multiple_of(r * 192, 192), 192), :] = field[:, lane * 128 : lane * 128 + 128]
+        for i in range(4):
+            re, im = w[i * HALF : i * HALF + HALF, :256], w[i * HALF : i * HALF + HALF, 256:]
+            v = jnp.concatenate([re * c - im * s, im * c + re * s], 0).astype(BF16)
+            field = dot(lh_ref[...], v) + dot(ll_ref[...], v)
+            for lane in range(2):
+                ys[lane, pl.ds(pl.multiple_of((step * 4 + i) * 192, 192), 192), :] = field[
+                    :, lane * 128 : lane * 128 + 128
+                ]
         return carry
 
-    lax.fori_loop(0, CYC, one_cycle, 0, unroll=2)
+    for copy in copies:
+        copy.wait()
+    lax.fori_loop(0, 4, four_cycles, 0)
+    leaving = []
     for a in range(SLOW):
         v = jnp.concatenate([ys.at[lane][pl.ds(a, CYC, stride=192), :] for lane in range(2)], 1)
         out_ref[:, FAST * a : FAST * a + FAST] = v[:, :FAST]
+        if a % 48 == 47 or a == SLOW - 1:
+            place = slice(FAST * (a // 48 * 48), FAST * a + FAST)
+            leaving.append(pltpu.make_async_copy(out_ref.at[:, place], out_hbm.at[:, place], osem.at[a // 48]))
+            leaving[-1].start()
+    for copy in leaving:
+        copy.wait()
 
 
 def inverse(msg, slots):
@@ -528,12 +557,19 @@
     return pl.pallas_call(
         inverse_kernel,
         out_shape=jax.ShapeDtypeStruct((CYC, LON), F32),
-        in_specs=[pl.BlockSpec(memory_space=pltpu.SMEM)] + [vmem()] * 5,
-        out_specs=vmem(),
+        in_specs=[pl.BlockSpec(memory_space=pltpu.SMEM), vmem()] + [pl.BlockSpec(memory_space=pl.ANY)] * 4,
+        out_specs=pl.BlockSpec(memory_space=pl.ANY),
         scratch_shapes=[
+            pltpu.VMEM((256, 512), BF16),
+            pltpu.VMEM((2, HALF, 256), F32),
+            pltpu.VMEM((192, 192), BF16),
+            pltpu.VMEM((192, 192), BF16),
+            pltpu.VMEM((CYC, LON), F32),
             pltpu.VMEM((TROWS, 128), F32),
             pltpu.VMEM((32 * 48, 128), F32),
             pltpu.VMEM((2, CYC * 192, 128), F32),
+            pltpu.SemaphoreType.DMA((4,)),
+            pltpu.SemaphoreType.DMA((4,)),
         ],
         compiler_params=pltpu.CompilerParams(vmem_limit_bytes=48 * MIB),
         name="inverse",

time: 90.2 us -> 83.3 us (0.924)
  Pallas kernels: 88.9 us -> 82 us
    pallas_call x1, Pallas kernels: 73.3 us -> 68.1 us  [main(): pl.pallas_call(main_kernel, out_shape=jax.ShapeDtypeStruct((16 * ROWS_OUT...]
    pallas_call x1, Pallas kernels: 15.7 us -> 13.9 us  [inverse(): pl.pallas_call(inverse_kernel, out_shape=jax.ShapeDtypeStruct((CYC, LON),...]
where the time goes in v6:
time: 83.3 us; the launch traced here: 83.1 us
  Pallas kernels  82 us (98%)
  local copies, waits for them, and re-layouts  1.01 us (1%)
    pallas_call x1, Pallas kernels, main(): pl.pallas_call(main_kernel, out_shape=jax.ShapeDtypeStruct((16 * ROWS_OUT...  68.1 us
    pallas_call x1, Pallas kernels, inverse(): pl.pallas_call(inverse_kernel, out_shape=jax.ShapeDtypeStruct((CYC, LON),...  13.9 us

profile of v6, /device:TPU:1, one launch (start us, length us, event | category | flops | bytes accessed | tf_op | source)
XLA Modules:
  0.0 83.1 jit_solution(11631043248418605524)
XLA Ops:
  0.0 0.0 copy-start.1
  0.0 0.0 copy-start.2
  0.0 0.0 copy-start.3
  0.0 0.0 copy-start.4
  0.0 0.0 copy-start.5
  0.0 68.1 %main.1.msg_ref = bf16[768,256]{1,0:T(8,128)(2,1)} custom-call(s32[5120]{0:T(1024)} %slot_ref.3, s32[320]{0:T(512)} %cut_ref.1, bf16[16,43200]{1,0:T(8,128)(2,1)} %x_hbm.1, bf16[192,192]{1,0:T(8,128)(2,1)} %constant.20.clone.fh_hbm, bf16[192,192]{1,0:T(8,128)(2,1)} %constant.21.clone.fl_hbm, f32[2,96,256]{2,1,0:T(8,128)} %constant.22.clone.twist_hbm, ...), custom_call_target="tpu_custom_call" | custom-call | flops 20000000000 | bytes 24000000 | tf_op jit(solution)/shard_map/main/pallas_call | solution.py:450
  68.1 0.0 copy-done.1
  68.2 0.0 copy-done.2
  68.2 0.0 copy-done.3
  68.2 0.0 copy-done.4
  68.2 0.0 copy-done.5
  68.2 0.0 copy-start
  68.2 1.0 %copy-done = bf16[768,256]{1,0:T(8,128)(2,1)S(1)} copy-done((bf16[768,256]{1,0:T(8,128)(2,1)S(1)}, bf16[768,256]{1,0:T(8,128)(2,1)}, u32[]{:S(2)}) %copy-start) | copy-done | bytes 393240
  69.2 13.9 %inverse.1 = f32[16,43200]{1,0:T(8,128)} custom-call(s32[5120]{0:T(1024)S(1)} %copy-done.5, bf16[768,256]{1,0:T(8,128)(2,1)S(1)} %copy-done, bf16[256,512]{1,0:T(8,128)(2,1)S(1)} %copy-done.1, f32[2,96,256]{2,1,0:T(8,128)S(1)} %copy-done.2, bf16[192,192]{1,0:T(8,128)(2,1)S(1)} %copy-done.4, bf16[192,192]{1,0:T(8,128)(2,1)S(1)} %copy-done.3), custom_call_target="tpu_custom_call" | custom-call | tf_op jit(solution)/shard_map/inverse/pallas_call | solution.py:557
Async XLA Ops:
  0.0 68.1 %copy-start.1 = (bf16[256,512]{1,0:T(8,128)(2,1)S(1)}, bf16[256,512]{1,0:T(8,128)(2,1)}, u32[]{:S(2)}) copy-start(bf16[256,512]{1,0:T(8,128)(2,1)} %constant.27.clone.back_hbm) | copy-start | bytes 786436
  0.0 68.2 %copy-start.2 = (f32[2,96,256]{2,1,0:T(8,128)S(1)}, f32[2,96,256]{2,1,0:T(8,128)}, u32[]{:S(2)}) copy-start(f32[2,96,256]{2,1,0:T(8,128)} %constant.22.clone.twist_hbm) | copy-start | bytes 589828
  0.0 68.2 %copy-start.3 = (bf16[192,192]{1,0:T(8,128)(2,1)S(1)}, bf16[192,192]{1,0:T(8,128)(2,1)}, u32[]{:S(2)}) copy-start(bf16[192,192]{1,0:T(8,128)(2,1)} %constant.29.clone.ll_hbm) | copy-start | bytes 221188
  0.0 68.2 %copy-start.4 = (bf16[192,192]{1,0:T(8,128)(2,1)S(1)}, bf16[192,192]{1,0:T(8,128)(2,1)}, u32[]{:S(2)}) copy-start(bf16[192,192]{1,0:T(8,128)(2,1)} %constant.28.clone.lh_hbm) | copy-start | bytes 221188
  0.0 68.2 %copy-start.5 = (s32[5120]{0:T(1024)S(1)}, s32[5120]{0:T(1024)}, u32[]{:S(2)}) copy-start(s32[5120]{0:T(1024)} %slot_ref.3) | copy-start | bytes 61444
  68.2 1.0 %copy-start = (bf16[768,256]{1,0:T(8,128)(2,1)S(1)}, bf16[768,256]{1,0:T(8,128)(2,1)}, u32[]{:S(2)}) copy-start(bf16[768,256]{1,0:T(8,128)(2,1)} %main.1.msg_ref) | copy-start | bytes 1179652

commit v7 on v6

--- a/solution.py
+++ b/solution.py
@@ -123,7 +123,7 @@
 def main_kernel(slot_ref, cut_ref, x_hbm, fh_hbm, fl_hbm, twist_hbm, second_hbm, panel_ref, diag_ref,
                 factor_ref, pick_ref, out_ref,
                 x_ref, fh_ref, fl_ref, twist_ref, second_ref, xs, qs, ts, gs, msg_ref,
-                pan, got, acc, mine, parts, coeff, keeps, wide, syn,
+                pan, got, mine, parts, coeff, keeps, wide, syn,
                 xsem, tsem, psem, s1, r1, s2, r2, s3, r3, s4, r4):
     lat = lax.axis_index("lat")
     me = lax.axis_index("ord")
@@ -139,16 +139,17 @@
         place = pl.ds(pl.multiple_of(behind(d) * 16, 16), 16)
         return pltpu.make_async_copy(panel_ref.at[place], pan.at[place], psem.at[d])
 
-    def in_copy(d):
+    base = (0, 256, 512)
+    share = (32, 32, 16)
+
+    def in_copy(T, d):
+        size = share[T]
         return pltpu.make_async_remote_copy(
-            src_ref=msg_ref.at[pl.ds(pl.multiple_of(ahead(d) * ROWS_IN, 16), ROWS_IN)],
-            dst_ref=got.at[pl.ds(pl.multiple_of(me * ROWS_IN, 16), ROWS_IN)],
-            send_sem=s1.at[d], recv_sem=r1.at[d],
+            src_ref=msg_ref.at[pl.ds(pl.multiple_of(ahead(d) * ROWS_IN + T * 32, 16), size)],
+            dst_ref=got.at[pl.ds(pl.multiple_of(me * ROWS_IN + T * 32, 16), size)],
+            send_sem=s1.at[T, d], recv_sem=r1.at[T, d],
             device_id=(lat, ahead(d)), device_id_type=MESH,
         )
-
-    base = (0, 256, 512)
-    share = (32, 32, 16)
 
     def slab_copy(T, d):
         peer = (lat + d) % 8
@@ -253,7 +254,7 @@
     for i in range(4):
         table_copy(i).wait()
     loop(0, 16, lambda d: panel_copy(d).start())
-    lax.fori_loop(0, CYC, one_cycle, 0, unroll=2)
+    lax.fori_loop(0, CYC, one_cycle, 0, unroll=4)
 
     def one_k(k, carry):
         t = qs[pl.ds(k * 128 if isinstance(k, int) else pl.multiple_of(k * 128, 128), 128), :].T
@@ -277,45 +278,69 @@
 
     sub = lax.broadcasted_iota(jnp.int32, (8, 128), 0)
 
-    def one_chip(i, carry):
+    def chip_of(i):
         far = 7 - i // 2 - i % 2 * 4
-        chip = (hy + far // 4) % 2 * 4 + (hz + far % 4) % 4
-        for j in range(5):
-            tile = chip * 5 + j
-            for i in range(0, 128, 32):
-                rows = [ts[pl.ds(slot_ref[tile * 128 + i + e] + 1, 1), :] for e in range(32)]
-                for e in range(32):
-                    gs[j, i + e : i + e + 1, :] = rows[e]
-            t = gs[j].T
-            sides = [swap_chunks([t[(h * 8 + r) * 8 : (h * 8 + r + 1) * 8] for r in range(8)]) for h in range(2)]
-            rows = []
-            for u in (0, 4):
-                for side in sides:
-                    rows.append(
-                        jnp.concatenate(
-                            [jnp.where(sub < 6, side[u + v], pltpu.roll(side[u + 3], 6 - 2 * v, 0)) for v in range(3)], 1
-                        )
-                    )
-            msg_ref[pl.ds(pl.multiple_of(tile * 32, 32), 32), :] = jnp.concatenate(rows, 0).astype(BF16)
-
+        return far, (hy + far // 4) % 2 * 4 + (hz + far % 4) % 4
+
+    def gathered(j, starts):
+        for i in range(0, 128, 32):
+            at = starts[i // 64] + i % 64
+            rows = [ts[pl.ds(slot_ref[at + e] + 1, 1), :] for e in range(32)]
+            for e in range(32):
+                gs[j, i + e : i + e + 1, :] = rows[e]
+        t = gs[j].T
+        sides = [swap_chunks([t[(h * 8 + r) * 8 : (h * 8 + r + 1) * 8] for r in range(8)]) for h in range(2)]
+        blocks = []
+        for u in (0, 4):
+            packed = [
+                jnp.concatenate(
+                    [jnp.where(sub < 6, side[u + v], pltpu.roll(side[u + 3], 6 - 2 * v, 0)) for v in range(3)], 1
+                )
+                for side in sides
+            ]
+            blocks.append(jnp.concatenate(packed, 0).astype(BF16))
+        return blocks
+
+    def send(T, far):
         @pl.when(far > 0)
         def _():
-            in_copy(far * 2).start()
-
-        in_copy(far * 2 + 1).start()
+            in_copy(T, far * 2).start()
+
+        in_copy(T, far * 2 + 1).start()
+
+    for T in range(2):
+        def two_chips(step, carry):
+            for e in range(2):
+                far, chip = chip_of(step * 2 + e)
+                for j in range(2):
+                    to = chip * 2 + j
+                    start = to * 320 + T * 128
+                    blocks = gathered(e * 2 + j, (start, start + 64))
+                    msg_ref[pl.ds(pl.multiple_of(to * ROWS_IN + T * 32, 16), 32), :] = jnp.concatenate(blocks, 0)
+                send(T, far)
+            return carry
+
+        lax.fori_loop(0, 4, two_chips, 0)
+
+    def four_chips(step, carry):
+        for e in range(4):
+            far, chip = chip_of(step * 4 + e)
+            start = chip * 640 + 256
+            for j, block in enumerate(gathered(e, (start, start + 320))):
+                msg_ref[pl.ds(pl.multiple_of((chip * 2 + j) * ROWS_IN + 64, 16), 16), :] = block
+            send(2, far)
         return carry
 
-    lax.fori_loop(0, 8, one_chip, 0)
+    lax.fori_loop(0, 2, four_chips, 0)
     own_in = pl.ds(pl.multiple_of(me * ROWS_IN, 16), ROWS_IN)
     got[own_in, :] = msg_ref[own_in, :]
     loop(0, 16, lambda d: panel_copy(d).wait())
-    def contract(q, far_set):
+    def contract(q):
         sums = []
         for pair in range(2):
             accs = [None, None]
-            for d in far_set:
-                peer = behind(d)
-                rows = got[pl.ds(pl.multiple_of(peer * ROWS_IN + q * 16, 16), 16), :].astype(F32)
+            for peer in range(16):
+                rows = got[pl.ds(pl.multiple_of(q * 16 + peer * ROWS_IN, 16), 16), :].astype(F32)
                 for e in range(2):
                     v = pair * 2 + e
                     sides = []
@@ -331,37 +356,23 @@
                     two = jnp.concatenate([one, one], 0).astype(BF16)
                     left = jnp.concatenate([two] * 8, 0) * diag_ref[...]
                     right = pan[
-                        pl.ds(pl.multiple_of(peer * 16, 16), 16), pl.ds(pl.multiple_of(q * 64 + v * 16, 16), 16), :
+                        peer * 16 : peer * 16 + 16, pl.ds(pl.multiple_of(q * 64 + v * 16, 16), 16), :
                     ].reshape(256, DEG)
                     t = dot(left, right)
                     accs[e] = t if accs[e] is None else accs[e] + t
             sums += accs
         return sums
 
-    early = (14, 15, 6, 7, 12, 13, 4, 5)
-    late = (10, 11, 2, 3, 8, 9, 0, 1)
-
-    def first_half(q):
-        for v, t in enumerate(contract(q, early)):
-            acc[pl.ds(pl.multiple_of(q * 512 + v * 128, 128), 128), :] = t
-
-    def second_half(T, q):
-        for v, t in enumerate(contract(q, late)):
-            t = t + acc[pl.ds(pl.multiple_of(q * 512 + v * 128, 128), 128), :]
+    def sum_slots(T, q):
+        for v, t in enumerate(contract(q)):
             rows = t.reshape(16, 8, DEG)
             for c in range(2):
                 row = base[T] + c * 4 * share[T] + (q - 2 * T) * 64 + v * 16
                 mine[pl.ds(pl.multiple_of(row, 16), 16), :] = jnp.sum(rows * factor_ref[c][None], axis=1)
 
-    for d in early:
-        in_copy(d).wait_recv()
-    loop(0, 5, first_half)
-    for d in late:
-        if d:
-            in_copy(d).wait_recv()
-
     def analyse_part(T):
-        loop(2 * T, min(2 * T + 2, 5), lambda q: second_half(T, q))
+        loop(1, 16, lambda d: in_copy(T, d).wait_recv())
+        loop(2 * T, min(2 * T + 2, 5), lambda q: sum_slots(T, q))
         loop(1, 8, lambda d: slab_copy(T, d).start())
 
     def total_part(T):
@@ -431,8 +442,8 @@
     total_part(2)
     synthesis_part(1)
     synthesis_part(2)
-    loop(1, 16, lambda d: in_copy(d).wait_send())
     for T in range(3):
+        loop(1, 16, lambda d: in_copy(T, d).wait_send())
         loop(1, 16, lambda d: out_copy(T, d).wait())
 
         def finish_lat(d):
@@ -461,18 +472,17 @@
             vec((2, CYC * 192, 128), F32),
             vec((48 * 128, 128), F32),
             vec((TROWS, 128), F32),
-            vec((5, 128, 128), F32),
+            vec((4, 128, 128), F32),
             vec((16 * ROWS_IN, 384), BF16),
             vec((256, 320, DEG), BF16),
             vec((16 * ROWS_IN, 384), BF16),
-            vec((20 * 128, DEG), F32),
             vec((640, DEG), F32),
             vec((640, DEG), F32),
             vec((640, DEG), BF16),
             vec((80, DEG), F32),
             vec((8 * DEG, 256), BF16),
             vec((16 * ROWS_OUT, 256), BF16),
-            dma, dma((4,)), dma((16,)), dma((16,)), dma((16,)), dma((3, 8)), dma((3, 8)), dma((3, 8)), dma((3, 8)),
+            dma, dma((4,)), dma((16,)), dma((3, 16)), dma((3, 16)), dma((3, 8)), dma((3, 8)), dma((3, 8)), dma((3, 8)),
             dma((3, 16)), dma((3, 16)),
         ],
         compiler_params=pltpu.CompilerParams(
@@ -483,11 +493,15 @@
     )(slots, cutoffs, heights, *t["first"], t["twist"], t["second"], panels, t["diag"], factors, t["pick"])
 
 
-def inverse_kernel(slot_ref, msg_ref, back_hbm, twist_hbm, lh_hbm, ll_hbm, out_hbm,
-                   back_ref, twist_ref, lh_ref, ll_ref, out_ref, ts, ls, ys, tsem, osem):
+def inverse_kernel(slot_ref, msg_hbm, back_hbm, twist_hbm, lh_hbm, ll_hbm, out_hbm,
+                   msg_ref, back_ref, twist_ref, lh_ref, ll_ref, out_ref, ts, ls, ys, tsem, osem, msem):
     held = ((back_hbm, back_ref), (twist_hbm, twist_ref), (lh_hbm, lh_ref), (ll_hbm, ll_ref))
     copies = [pltpu.make_async_copy(held[i][0], held[i][1], tsem.at[i]) for i in range(4)]
-    for copy in copies:
+    pieces = [
+        pltpu.make_async_copy(msg_hbm.at[i * 192 : i * 192 + 192], msg_ref.at[i * 192 : i * 192 + 192], msem.at[i])
+        for i in range(4)
+    ]
+    for copy in pieces + copies:
         copy.start()
     ts[0:8, :] = jnp.zeros((8, 128), F32)
     ts[ORDERS:TROWS, :] = jnp.zeros((TROWS - ORDERS, 128), F32)
@@ -502,7 +516,9 @@
                 ts[pl.ds(slot_ref[base + i] + 1, 1), 0:32] = t[i : i + 1]
         return carry
 
-    lax.fori_loop(0, 16, one_peer, 0)
+    for i in range(4):
+        pieces[i].wait()
+        lax.fori_loop(4 * i, 4 * i + 4, one_peer, 0)
 
     def one_k(k, carry):
         stack = []
@@ -557,9 +573,10 @@
     return pl.pallas_call(
         inverse_kernel,
         out_shape=jax.ShapeDtypeStruct((CYC, LON), F32),
-        in_specs=[pl.BlockSpec(memory_space=pltpu.SMEM), vmem()] + [pl.BlockSpec(memory_space=pl.ANY)] * 4,
+        in_specs=[pl.BlockSpec(memory_space=pltpu.SMEM)] + [pl.BlockSpec(memory_space=pl.ANY)] * 5,
         out_specs=pl.BlockSpec(memory_space=pl.ANY),
         scratch_shapes=[
+            pltpu.VMEM((16 * ROWS_OUT, 256), BF16),
             pltpu.VMEM((256, 512), BF16),
             pltpu.VMEM((2, HALF, 256), F32),
             pltpu.VMEM((192, 192), BF16),
@@ -570,8 +587,9 @@
             pltpu.VMEM((2, CYC * 192, 128), F32),
             pltpu.SemaphoreType.DMA((4,)),
             pltpu.SemaphoreType.DMA((4,)),
+            pltpu.SemaphoreType.DMA((4,)),
         ],
-        compiler_params=pltpu.CompilerParams(vmem_limit_bytes=48 * MIB),
+        compiler_params=pltpu.CompilerParams(vmem_limit_bytes=62 * MIB),
         name="inverse",
     )(slots, msg, t["back"], t["twist"], *t["last"])
 

time: 83.3 us -> 80.3 us (0.964)
  Pallas kernels: 82 us -> 79.8 us
  local copies, waits for them, and re-layouts: 1.01 us -> 0 us
    pallas_call x1, Pallas kernels: 68.1 us -> 65.5 us  [main(): pl.pallas_call(main_kernel, out_shape=jax.ShapeDtypeStruct((16 * ROWS_OUT...]
    unnamed x12 -> x0, local copies, waits for them, and re-layouts: 1.01 us -> none
where the time goes in v7:
time: 80.3 us; the launch traced here: 80 us
  Pallas kernels  79.8 us (99%)
    pallas_call x1, Pallas kernels, main(): pl.pallas_call(main_kernel, out_shape=jax.ShapeDtypeStruct((16 * ROWS_OUT...  65.5 us
    pallas_call x1, Pallas kernels, inverse(): pl.pallas_call(inverse_kernel, out_shape=jax.ShapeDtypeStruct((CYC, LON),...  14.4 us

profile of v7, /device:TPU:1, one launch (start us, length us, event | category | flops | bytes accessed | tf_op | source)
XLA Modules:
  0.0 80.0 jit_solution(7279444224709801320)
XLA Ops:
  0.0 65.5 %main.1.msg_hbm = bf16[768,256]{1,0:T(8,128)(2,1)} custom-call(s32[5120]{0:T(1024)} %slot_ref.3, s32[320]{0:T(512)} %cut_ref.1, bf16[16,43200]{1,0:T(8,128)(2,1)} %x_hbm.1, bf16[192,192]{1,0:T(8,128)(2,1)} %constant.20.clone.fh_hbm, bf16[192,192]{1,0:T(8,128)(2,1)} %constant.21.clone.fl_hbm, f32[2,96,256]{2,1,0:T(8,128)} %constant.22.clone.twist_hbm, ...), custom_call_target="tpu_custom_call" | custom-call | flops 20000000000 | bytes 24000000 | tf_op jit(solution)/shard_map/main/pallas_call | solution.py:461
  65.5 14.4 %inverse.1 = f32[16,43200]{1,0:T(8,128)} custom-call(s32[5120]{0:T(1024)} %slot_ref.3, bf16[768,256]{1,0:T(8,128)(2,1)} %main.1.msg_hbm, bf16[256,512]{1,0:T(8,128)(2,1)} %constant.27.clone.back_hbm, f32[2,96,256]{2,1,0:T(8,128)} %constant.22.clone.twist_hbm, bf16[192,192]{1,0:T(8,128)(2,1)} %constant.28.clone.lh_hbm, bf16[192,192]{1,0:T(8,128)(2,1)} %constant.29.clone.ll_hbm), custom_call_target="tpu_custom_call" | custom-call | tf_op jit(solution)/shard_map/inverse/pallas_call | solution.py:573

commit v8 on v7

--- a/solution.py
+++ b/solution.py
@@ -18,6 +18,7 @@
 NMAX = 21600
 CYC = 16
 TROWS = 6016
+FIRST = 8
 F32 = jnp.float32
 BF16 = jnp.bfloat16
 MIB = 1024 * 1024
@@ -184,8 +185,15 @@
             return carry
         lax.fori_loop(low, high, step, 0)
 
-    heights_copy = pltpu.make_async_copy(x_hbm, x_ref, xsem)
-    heights_copy.start()
+    cuts = (0, 11520, 23040, 34560, LON)
+    heights = [
+        pltpu.make_async_copy(
+            x_hbm.at[:, cuts[i] : cuts[i + 1]], x_ref.at[:, cuts[i] : cuts[i + 1]], xsem.at[i]
+        )
+        for i in range(4)
+    ]
+    for copy in heights:
+        copy.start()
     held = ((fh_hbm, fh_ref), (fl_hbm, fl_ref), (twist_hbm, twist_ref), (second_hbm, second_ref))
 
     def table_copy(i):
@@ -203,7 +211,7 @@
             slot = T * 128 + (lat * size + i) % (4 * size)
             row = T * 32 + i
             keeps[row : row + 1, :] = jnp.where(degree <= cut_ref[slot], 1.0, 0.0)
-    heights_copy.wait()
+    landed = 0
     inside = lax.broadcasted_iota(jnp.int32, (CYC, 256), 1) < FAST
     for r in range(CYC):
         for lane in range(2):
@@ -211,6 +219,10 @@
     for a in range(SLOW):
         start = FAST * a // 128 * 128
         off = FAST * a - start
+        while landed < min(start + 384, LON):
+            i = cuts.index(landed)
+            heights[i].wait()
+            landed = cuts[i + 1]
         if start + 384 <= LON:
             v = x_ref[:, start : start + 384].astype(F32)
         else:
@@ -258,14 +270,14 @@
 
     def one_k(k, carry):
         t = qs[pl.ds(k * 128 if isinstance(k, int) else pl.multiple_of(k * 128, 128), 128), :].T
-        ts[pl.ds(k, 32, stride=SLOW), :] = t[0:32]
-        ts[pl.ds(SLOW - k, 32, stride=SLOW), :] = t[32:64]
+        ts[pl.ds(k + FIRST - 1, 32, stride=SLOW), :] = t[0:32]
+        ts[pl.ds(SLOW - k + FIRST - 1, 32, stride=SLOW), :] = t[32:64]
         return t
 
     def two_k(k, carry):
         t = one_k(k, carry)
-        ts[pl.ds(k + 48, 32, stride=SLOW), :] = t[64:96]
-        ts[pl.ds(SLOW - 48 - k, 32, stride=SLOW), :] = t[96:128]
+        ts[pl.ds(k + 48 + FIRST - 1, 32, stride=SLOW), :] = t[64:96]
+        ts[pl.ds(SLOW - 48 - k + FIRST - 1, 32, stride=SLOW), :] = t[96:128]
         return carry
 
     lax.fori_loop(0, 40, two_k, 0, unroll=4)
@@ -278,6 +290,8 @@
 
     sub = lax.broadcasted_iota(jnp.int32, (8, 128), 0)
 
+    orders = ts.at[pl.ds(FIRST, ORDERS)]
+
     def chip_of(i):
         far = 7 - i // 2 - i % 2 * 4
         return far, (hy + far // 4) % 2 * 4 + (hz + far % 4) % 4
@@ -285,7 +299,7 @@
     def gathered(j, starts):
         for i in range(0, 128, 32):
             at = starts[i // 64] + i % 64
-            rows = [ts[pl.ds(slot_ref[at + e] + 1, 1), :] for e in range(32)]
+            rows = [orders[pl.ds(slot_ref[at + e], 1), :] for e in range(32)]
             for e in range(32):
                 gs[j, i + e : i + e + 1, :] = rows[e]
         t = gs[j].T
@@ -482,7 +496,7 @@
             vec((80, DEG), F32),
             vec((8 * DEG, 256), BF16),
             vec((16 * ROWS_OUT, 256), BF16),
-            dma, dma((4,)), dma((16,)), dma((3, 16)), dma((3, 16)), dma((3, 8)), dma((3, 8)), dma((3, 8)), dma((3, 8)),
+            dma((4,)), dma((4,)), dma((16,)), dma((3, 16)), dma((3, 16)), dma((3, 8)), dma((3, 8)), dma((3, 8)), dma((3, 8)),
             dma((3, 16)), dma((3, 16)),
         ],
         compiler_params=pltpu.CompilerParams(
@@ -503,8 +517,9 @@
     ]
     for copy in pieces + copies:
         copy.start()
-    ts[0:8, :] = jnp.zeros((8, 128), F32)
-    ts[ORDERS:TROWS, :] = jnp.zeros((TROWS - ORDERS, 128), F32)
+    ts[0:FIRST, :] = jnp.zeros((FIRST, 128), F32)
+    ts[FIRST + ORDERS : TROWS, :] = jnp.zeros((TROWS - ORDERS - FIRST, 128), F32)
+    orders = ts.at[pl.ds(FIRST, ORDERS)]
 
     def one_peer(o, carry):
         for part in range(3):
@@ -513,7 +528,7 @@
             t = jnp.concatenate([rows[:, :128], rows[:, 128:]], 0).T
             base = o * 320 + part * 128
             for i in range(count):
-                ts[pl.ds(slot_ref[base + i] + 1, 1), 0:32] = t[i : i + 1]
+                orders[pl.ds(slot_ref[base + i], 1), 0:32] = t[i : i + 1]
         return carry
 
     for i in range(4):
@@ -523,8 +538,8 @@
     def one_k(k, carry):
         stack = []
         for base in (0, 48):
-            plus = ts[pl.ds(k + base, 32, stride=SLOW), :]
-            minus = ts[pl.ds(SLOW - base - k, 32, stride=SLOW), :]
+            plus = ts[pl.ds(k + base + FIRST - 1, 32, stride=SLOW), :]
+            minus = ts[pl.ds(SLOW - base - k + FIRST - 1, 32, stride=SLOW), :]
             lone = k == 0 if base == 0 else k == 90 - base
             stack += [plus, jnp.where(lone, 0.0, minus)]
         ls[pl.ds(k, 32, stride=48), :] = jnp.concatenate(stack, 0)[:, :32].T

time: 80.3 us -> 79.9 us (level)
  no operation moved by 1% of the time
where the time goes in v8:
time: 79.9 us; the launch traced here: 79.6 us
  Pallas kernels  79.4 us (99%)
    pallas_call x1, Pallas kernels, main(): pl.pallas_call(main_kernel, out_shape=jax.ShapeDtypeStruct((16 * ROWS_OUT...  65.1 us
    pallas_call x1, Pallas kernels, inverse(): pl.pallas_call(inverse_kernel, out_shape=jax.ShapeDtypeStruct((CYC, LON),...  14.4 us

profile of v8, /device:TPU:1, one launch (start us, length us, event | category | flops | bytes accessed | tf_op | source)
XLA Modules:
  0.0 79.6 jit_solution(13130044009559215882)
XLA Ops:
  0.0 65.1 %main.1.msg_hbm = bf16[768,256]{1,0:T(8,128)(2,1)} custom-call(s32[5120]{0:T(1024)} %slot_ref.3, s32[320]{0:T(512)} %cut_ref.1, bf16[16,43200]{1,0:T(8,128)(2,1)} %x_hbm.1, bf16[192,192]{1,0:T(8,128)(2,1)} %constant.20.clone.fh_hbm, bf16[192,192]{1,0:T(8,128)(2,1)} %constant.21.clone.fl_hbm, f32[2,96,256]{2,1,0:T(8,128)} %constant.22.clone.twist_hbm, ...), custom_call_target="tpu_custom_call" | custom-call | flops 20000000000 | bytes 24000000 | tf_op jit(solution)/shard_map/main/pallas_call | solution.py:475
  65.1 14.4 %inverse.1 = f32[16,43200]{1,0:T(8,128)} custom-call(s32[5120]{0:T(1024)} %slot_ref.3, bf16[768,256]{1,0:T(8,128)(2,1)} %main.1.msg_hbm, bf16[256,512]{1,0:T(8,128)(2,1)} %constant.27.clone.back_hbm, f32[2,96,256]{2,1,0:T(8,128)} %constant.22.clone.twist_hbm, bf16[192,192]{1,0:T(8,128)(2,1)} %constant.28.clone.lh_hbm, bf16[192,192]{1,0:T(8,128)(2,1)} %constant.29.clone.ll_hbm), custom_call_target="tpu_custom_call" | custom-call | tf_op jit(solution)/shard_map/inverse/pallas_call | solution.py:588

commit v9 on v8

--- a/solution.py
+++ b/solution.py
@@ -533,7 +533,7 @@
 
     for i in range(4):
         pieces[i].wait()
-        lax.fori_loop(4 * i, 4 * i + 4, one_peer, 0)
+        lax.fori_loop(4 * i, 4 * i + 4, one_peer, 0, unroll=2)
 
     def one_k(k, carry):
         stack = []
@@ -570,7 +570,7 @@
 
     for copy in copies:
         copy.wait()
-    lax.fori_loop(0, 4, four_cycles, 0)
+    lax.fori_loop(0, 4, four_cycles, 0, unroll=2)
     leaving = []
     for a in range(SLOW):
         v = jnp.concatenate([ys.at[lane][pl.ds(a, CYC, stride=192), :] for lane in range(2)], 1)

time: 79.9 us -> 79.4 us (level)
  no operation moved by 1% of the time
where the time goes in v9:
time: 79.4 us; the launch traced here: 79.1 us
  Pallas kernels  78.9 us (99%)
    pallas_call x1, Pallas kernels, main(): pl.pallas_call(main_kernel, out_shape=jax.ShapeDtypeStruct((16 * ROWS_OUT...  65.1 us
    pallas_call x1, Pallas kernels, inverse(): pl.pallas_call(inverse_kernel, out_shape=jax.ShapeDtypeStruct((CYC, LON),...  13.9 us

profile of v9, /device:TPU:1, one launch (start us, length us, event | category | flops | bytes accessed | tf_op | source)
XLA Modules:
  0.0 79.1 jit_solution(4451394212354705757)
XLA Ops:
  0.0 65.1 %main.1.msg_hbm = bf16[768,256]{1,0:T(8,128)(2,1)} custom-call(s32[5120]{0:T(1024)} %slot_ref.3, s32[320]{0:T(512)} %cut_ref.1, bf16[16,43200]{1,0:T(8,128)(2,1)} %x_hbm.1, bf16[192,192]{1,0:T(8,128)(2,1)} %constant.20.clone.fh_hbm, bf16[192,192]{1,0:T(8,128)(2,1)} %constant.21.clone.fl_hbm, f32[2,96,256]{2,1,0:T(8,128)} %constant.22.clone.twist_hbm, ...), custom_call_target="tpu_custom_call" | custom-call | flops 20000000000 | bytes 24000000 | tf_op jit(solution)/shard_map/main/pallas_call | solution.py:475
  65.1 13.9 %inverse.1 = f32[16,43200]{1,0:T(8,128)} custom-call(s32[5120]{0:T(1024)} %slot_ref.3, bf16[768,256]{1,0:T(8,128)(2,1)} %main.1.msg_hbm, bf16[256,512]{1,0:T(8,128)(2,1)} %constant.27.clone.back_hbm, f32[2,96,256]{2,1,0:T(8,128)} %constant.22.clone.twist_hbm, bf16[192,192]{1,0:T(8,128)(2,1)} %constant.28.clone.lh_hbm, bf16[192,192]{1,0:T(8,128)(2,1)} %constant.29.clone.ll_hbm), custom_call_target="tpu_custom_call" | custom-call | tf_op jit(solution)/shard_map/inverse/pallas_call | solution.py:588
